TPU v7x, 128 devices: a whole 4x4x4 slice. The times are simulated.
128 devices in a mesh: row: 8 (over y_hi, x), col: 16 (over y_lo, z, core).
Axes of the slice: x: 4, y: 4 (y_hi: 2, y_lo: 2; y = y_hi * 2 + y_lo), z: 4, core: 2. Of those that a mesh axis runs over, the one named last changes fastest.
Arguments:
- replay_pool: bfloat16 [8192, 512], P('row'), may hold values from -6 to 6
- sample_ids: int32 [8, 1024], P('row'), may hold values from 0 to 1023, each once within a row
- rotation_bins: int32 [8192], P('row'), may hold values from 0 to 15
Outputs:
- factored: float32 [8192, 8192], P('row', 'col')
Inputs may be any that keep to these rules, and one draw needn't show every extreme that they name: Each row of sample_ids is a permutation of 0 to 1023.
All inputs are finite; a program needn't handle non-finite values.
Results may differ from a plain program's by a relative error of at most 0.0003.
Values may be sent and summed in bfloat16 or wider, within the bound.
A program may use at most 128 MiB of HBM per device.

v0:
```python
import jax
import jax.numpy as jnp
from jax import lax
from jax.sharding import PartitionSpec as P

ROTS = 16


sharpness = 2.0
ridge_weight = 0.1
highest = lax.Precision.HIGHEST


def from_root(x, axis, root):
    mine = lax.axis_index(axis) == root
    return lax.psum(jnp.where(mine, x, jnp.zeros_like(x)), axis)


def orbit_kernel(row_feats, row_rot, row_global, col_feats, col_rot, col_global):
    feat_width = row_feats.shape[1]
    rotations = ROTS
    row_norms = jnp.sum(jnp.square(row_feats.astype(jnp.float32)), axis=1)
    col_norms = jnp.sum(jnp.square(col_feats.astype(jnp.float32)), axis=1)
    col_binned = col_feats.reshape(col_feats.shape[0], rotations, feat_width // rotations)
    summed = jnp.zeros((row_feats.shape[0], col_feats.shape[0]), jnp.float32)
    for rotation in range(rotations):
        rolled = jnp.roll(col_binned, rotation, axis=1).reshape(col_feats.shape[0], feat_width)
        products = jnp.einsum("nf,mf->nm", row_feats, rolled, preferred_element_type=jnp.float32)
        distance = row_norms[:, None] + col_norms[None, :] - 2.0 * products
        summed = summed + jnp.exp(-distance / feat_width)
    bin_gap = (row_rot[:, None] - col_rot[None, :]).astype(jnp.float32)
    weight = jnp.exp(sharpness * (jnp.cos(bin_gap * (2.0 * jnp.pi / rotations)) - 1.0))
    same_point = (row_global[:, None] == col_global[None, :]).astype(jnp.float32)
    return weight * summed / rotations + ridge_weight * same_point


def per_device(replay_pool, sample_ids, rotation_bins):
    rows_here = lax.axis_size("row")
    cols_here = lax.axis_size("col")
    row_index = lax.axis_index("row")
    column_index = lax.axis_index("col")
    rows_dev = replay_pool.shape[0]
    block_rows = rows_dev // rows_here
    block_cols = rows_dev // cols_here
    cols_dev = block_cols * rows_here
    features = replay_pool[sample_ids[0]]
    col_start = column_index * block_cols
    col_piece = lax.dynamic_slice_in_dim(features, col_start, block_cols, 0)
    col_rot_piece = lax.dynamic_slice_in_dim(rotation_bins, col_start, block_cols, 0)
    col_feats, col_rot = (
        lax.all_gather(col_piece, "row", axis=0, tiled=True),
        lax.all_gather(col_rot_piece, "row", axis=0, tiled=True),
    )
    cycles = jnp.arange(rows_here, dtype=jnp.int32)[:, None]
    col_global = (
        (cycles * cols_here + column_index) * block_cols
        + jnp.arange(block_cols, dtype=jnp.int32)[None, :]
    ).reshape(cols_dev)
    row_global = row_index * rows_dev + jnp.arange(rows_dev, dtype=jnp.int32)
    local_tile = orbit_kernel(features, rotation_bins, row_global, col_feats, col_rot, col_global)
    kernel_tile = lax.all_to_all(local_tile, "row", split_axis=0, concat_axis=0, tiled=True)
    panel_columns = lax.all_gather(kernel_tile[:, :block_cols], "col", axis=1, tiled=True)
    pieces = lax.all_gather(
        kernel_tile[None, :block_rows, :block_cols], ("row", "col"), axis=0, tiled=True
    )
    diag_block = (
        pieces.reshape(rows_here, cols_here, block_rows, block_cols)
        .transpose(0, 2, 1, 3)
        .reshape(rows_dev, rows_dev)
    )
    diag_factor = jnp.linalg.cholesky(diag_block)
    panel = jax.scipy.linalg.solve_triangular(diag_factor, panel_columns.T, lower=True).T
    ratio = cols_here // rows_here
    source = column_index // ratio
    grouped = panel.reshape(rows_here, ratio, block_cols, panel.shape[1])
    picked = lax.dynamic_index_in_dim(
        grouped, column_index % ratio, axis=1, keepdims=False
    ).reshape(cols_dev, panel.shape[1])
    col_panel = from_root(picked, "row", source)[block_cols:]
    trailing = kernel_tile[:, block_cols:] - jnp.einsum(
        "nk,mk->nm", panel, col_panel, precision=highest
    )
    leading = lax.dynamic_slice_in_dim(panel, col_start, block_cols, 1)
    return jnp.concatenate([leading, trailing], axis=1)


def solution(mesh):
    in_specs = (P("row", None), P("row", None), P("row"))
    out_specs = P("row", "col")
    return jax.shard_map(
        per_device, mesh=mesh, in_specs=in_specs, out_specs=out_specs, check_vma=False
    )
```

profile of v0, /device:TPU:102, one launch (start us, length us, event | category | flops | bytes accessed | tf_op | source)
XLA Modules:
  0.0 812.6 jit_solution(12275747941705651215)
XLA Ops:
  12.0 35.1 %all_gather.13 = bf16[512,512]{1,0:T(8,128)(2,1)S(1)} all-gather(bf16[64,512]{1,0:T(8,128)(2,1)S(1)} %constant_dynamic-slice_fusion.1), channel_id=1, replica_groups=mesh['row'=8,'col'=16] {'row'}, dimensions={0}, use_global_device_ids=true | all-gather | bytes 589824 | tf_op jit(solution)/shard_map/all_gather | solution.py:51
  63.2 10.7 %all-reduce.1 = s32[512]{0:T(512)S(1)} all-reduce(s32[512]{0:T(512)S(1)} %dynamic-slice_dynamic-update-slice_fusion), channel_id=1, replica_groups=mesh['row'=8,'col'=16] {'row'}, use_global_device_ids=true, to_apply=%add.1 | all-reduce | flops 512 | bytes 4096
  90.1 15.0 %select_add_fusion = f32[1024,512]{1,0:T(8,128)S(1)} fusion(f32[1024,512]{1,0:T(8,128)S(1)} %fusion.168, f32[1024,512]{1,0:T(8,128)S(1)} %fusion.167, f32[1024,512]{1,0:T(8,128)S(1)} %fusion.166, f32[1024,512]{1,0:T(8,128)S(1)} %fusion.165, f32[1024,512]{1,0:T(8,128)S(1)} %fusion.164, f32[1024,512]{1,0:T(8,128)S(1)} %fusion.163, ...), kind=kOutput, calls=%fused_computation.98 | convolution fusion | flops 584056832 | bytes 35145728 | tf_op jit(solution)/shard_map/nf,mf->nm/dot_general | solution.py:28
  105.1 23.3 %all_to_all.12 = f32[8,128,512]{2,1,0:T(8,128)S(1)} all-to-all(f32[8,128,512]{2,1,0:T(8,128)S(1)} %bitcast.212), channel_id=1, replica_groups=mesh['row'=8,'col'=16] {'row'}, dimensions={0} | all-to-all | bytes 4194304 | tf_op jit(solution)/shard_map/all_to_all | solution.py:61
  130.3 201.7 %all-gather.6.cloned.1.call-done = f32[16384,64]{0,1:T(8,128)} async-done(((f32[128,64]{0,1:T(8,128)}), f32[16384,64]{0,1:T(8,128)}) %all-gather.6.cloned.1.call-update) | async-done | bytes 4194320 | tf_op jit(solution)/shard_map/all_gather | solution.py:63
  352.1 11.7 %cholesky.223 = f32[128,128]{1,0:T(8,128)S(1)} custom-call(f32[128,128]{1,0:T(8,128)S(1)} %cholesky.580), custom_call_target="Cholesky" | custom-call | tf_op jit(solution)/shard_map/jit(cholesky)/cholesky | solution.py:71
  363.8 9.8 %custom-call.63 = f32[1,128,128]{1,2,0:T(8,128)S(1)} custom-call(f32[1,128,128]{2,1,0:T(8,128)S(1)} %get-tuple-element.99), custom_call_target="InvertDiagBlocksLowerTriangular" | custom-call | tf_op jit(solution)/shard_map/jit(cholesky)/cholesky | solution.py:71
  380.1 11.9 %cholesky.244 = f32[128,128]{1,0:T(8,128)S(1)} custom-call(f32[128,128]{1,0:T(8,128)S(1)} %cholesky.584), custom_call_target="Cholesky" | custom-call | tf_op jit(solution)/shard_map/jit(cholesky)/cholesky | solution.py:71
  392.6 9.8 %custom-call.64 = f32[1,128,128]{1,2,0:T(8,128)S(1)} custom-call(f32[1,128,128]{2,1,0:T(8,128)S(1)} %get-tuple-element.96), custom_call_target="InvertDiagBlocksLowerTriangular" | custom-call | tf_op jit(solution)/shard_map/jit(cholesky)/cholesky | solution.py:71
  405.7 11.7 %cholesky.468 = f32[128,128]{1,0:T(8,128)S(1)} custom-call(f32[128,128]{1,0:T(8,128)S(1)} %cholesky.589), custom_call_target="Cholesky" | custom-call | tf_op jit(solution)/shard_map/jit(cholesky)/cholesky | solution.py:71
  418.1 9.8 %custom-call.65 = f32[1,128,128]{1,2,0:T(8,128)S(1)} custom-call(f32[1,128,128]{2,1,0:T(8,128)S(1)} %get-tuple-element.93), custom_call_target="InvertDiagBlocksLowerTriangular" | custom-call | tf_op jit(solution)/shard_map/jit(cholesky)/cholesky | solution.py:71
  431.4 12.1 %cholesky.487 = f32[128,128]{1,0:T(8,128)S(1)} custom-call(f32[128,128]{1,0:T(8,128)S(1)} %cholesky.594), custom_call_target="Cholesky" | custom-call | tf_op jit(solution)/shard_map/jit(cholesky)/cholesky | solution.py:71
  444.2 9.8 %custom-call.66 = f32[1,128,128]{1,2,0:T(8,128)S(1)} custom-call(f32[1,128,128]{2,1,0:T(8,128)S(1)} %get-tuple-element.90), custom_call_target="InvertDiagBlocksLowerTriangular" | custom-call | tf_op jit(solution)/shard_map/jit(cholesky)/cholesky | solution.py:71
  457.5 11.7 %cholesky.506 = f32[128,128]{1,0:T(8,128)S(1)} custom-call(f32[128,128]{1,0:T(8,128)S(1)} %cholesky.599), custom_call_target="Cholesky" | custom-call | tf_op jit(solution)/shard_map/jit(cholesky)/cholesky | solution.py:71
  469.9 10.0 %custom-call.67 = f32[1,128,128]{1,2,0:T(8,128)S(1)} custom-call(f32[1,128,128]{2,1,0:T(8,128)S(1)} %get-tuple-element.87), custom_call_target="InvertDiagBlocksLowerTriangular" | custom-call | tf_op jit(solution)/shard_map/jit(cholesky)/cholesky | solution.py:71
  483.2 11.7 %cholesky.526 = f32[128,128]{1,0:T(8,128)S(1)} custom-call(f32[128,128]{1,0:T(8,128)S(1)} %cholesky.604), custom_call_target="Cholesky" | custom-call | tf_op jit(solution)/shard_map/jit(cholesky)/cholesky | solution.py:71
  495.5 9.8 %custom-call.68 = f32[1,128,128]{1,2,0:T(8,128)S(1)} custom-call(f32[1,128,128]{2,1,0:T(8,128)S(1)} %get-tuple-element.84), custom_call_target="InvertDiagBlocksLowerTriangular" | custom-call | tf_op jit(solution)/shard_map/jit(cholesky)/cholesky | solution.py:71
  508.3 11.9 %cholesky.546 = f32[128,128]{1,0:T(8,128)S(1)} custom-call(f32[128,128]{1,0:T(8,128)S(1)} %cholesky.609), custom_call_target="Cholesky" | custom-call | tf_op jit(solution)/shard_map/jit(cholesky)/cholesky | solution.py:71
  520.9 9.8 %custom-call.69 = f32[1,128,128]{1,2,0:T(8,128)S(1)} custom-call(f32[1,128,128]{2,1,0:T(8,128)S(1)} %get-tuple-element.81), custom_call_target="InvertDiagBlocksLowerTriangular" | custom-call | tf_op jit(solution)/shard_map/jit(cholesky)/cholesky | solution.py:71
  533.4 11.7 %cholesky.564 = f32[128,128]{1,0:T(8,128)S(1)} custom-call(f32[128,128]{1,0:T(8,128)S(1)} %convolution_subtract_fusion.11), custom_call_target="Cholesky" | custom-call | tf_op jit(solution)/shard_map/jit(cholesky)/cholesky | solution.py:71
  561.0 23.4 %while.1 = (s32[]{:T(128)}, f32[1024,1024]{1,0:T(8,128)}, s32[8,2]{0,1:T(2,128)S(1)}, f32[8,128,128]{2,1,0:T(8,128)S(1)}, s32[]{:T(128)}) while((s32[]{:T(128)}, f32[1024,1024]{1,0:T(8,128)}, s32[8,2]{0,1:T(2,128)S(1)}, f32[8,128,128]{2,1,0:T(8,128)S(1)}, s32[]{:T(128)}) %tuple.77), condition=%wide.while_cond, body=%wide.while_body.sunk | while | flops 2 | bytes 131189 | solution.py:72
  584.4 79.0 %custom-call.70 = f32[8,128,128]{1,2,0:T(8,128)S(1)} custom-call(f32[8,128,128]{2,1,0:T(8,128)S(1)} %get-tuple-element.12), custom_call_target="InvertDiagBlocksLowerTriangular" | custom-call | tf_op jit(solution)/shard_map/jit(_solve_triangular)/triangular_solve | solution.py:72
  706.6 86.3 %all-reduce.4.cloned.1.call-done = f32[512,1024]{1,0:T(8,128)} async-done(((f32[512,1024]{1,0:T(8,128)}), f32[512,1024]{1,0:T(8,128)}) %all-reduce.4.cloned.1.call-update) | async-done | bytes 2097168 | tf_op jit(solution)/shard_map/psum | solution.py:16
  792.8 8.7 %fusion.81 = f32[1024,448]{0,1:T(8,128)S(1)} fusion(f32[1024,448]{0,1:T(8,128)S(1)} %copy.17, f32[1024,1024]{1,0:T(8,128)} %convolution_dynamic-update-slice_fusion, f32[512,1024]{1,0:T(8,128)} %all-reduce.4.cloned.1.call-done), kind=kOutput, calls=%fused_computation.108 | convolution fusion | flops 5637603328 | bytes 9699328 | tf_op jit(solution)/shard_map/nk,mk->nm/dot_general | solution.py:80
  (219 shorter events, 169.8 us)
Async XLA Ops:
  6.5 1.2 copy-start
  6.5 325.4 %all-gather.6.cloned.1.call-start = ((), (), s32[]{:S(2)}) async-start(), calls=%async_computation.3 | async-start | bytes 4227072 | tf_op jit(solution)/shard_map/all_gather | solution.py:63
  59.0 2.2 copy-start.30
  77.5 1.1 copy-start.7
  77.5 1.1 copy-start.26
  77.5 1.2 copy-start.27
  79.4 1.1 copy-start.9
  79.5 1.1 copy-start.24
  79.5 1.2 copy-start.25
  81.4 1.1 copy-start.22
  81.4 1.2 copy-start.23
  83.4 1.1 copy-start.20
  83.4 1.2 copy-start.21
  85.4 1.1 copy-start.18
  85.4 1.2 copy-start.19
  88.1 1.1 copy-start.28
  88.5 1.6 copy-start.5
  88.5 1.6 copy-start.29
  129.1 534.3 %all-gather.4.cloned.1.call-start = ((), (), s32[]{:S(2)}) async-start(), calls=%async_computation.1 | async-start | bytes 4456448 | tf_op jit(solution)/shard_map/all_gather | solution.py:62
  130.2 662.6 %all-reduce.4.cloned.1.call-start = ((), (), s32[]{:S(2)}) async-start(), calls=%async_computation.2 | async-start | bytes 4194304 | tf_op jit(solution)/shard_map/psum | solution.py:16
  336.3 3.2 copy-start.2
  350.1 2.0 copy-start.3
  666.0 3.4 copy-start.4
  801.5 4.4 copy-start.1
  (10 other events, 10.1 us)
Sparse Core Ops, SparseCore 0:
  129.2 202.6 all-gather.5
  333.7 36.9 all-gather.3
  701.9 90.9 all-reduce.3
where the time goes:
time: 820 us; the launch traced here: 813 us
  waiting for transfers between devices  288 us (35%)
  other arithmetic  271 us (33%)
  matrix products  88.3 us (11%)
  local copies, waits for them, and re-layouts  76.5 us (9%)
  blocking collectives  69.1 us (8%)
  between operations  19.7 us (2%)
    all_gather x1, waiting for transfers between devices, per_device(): lax.all_gather(kernel_tile[None, :block_rows, :block_cols], ('row', 'col'...  202 us
    another operation x31, other arithmetic, per_device(): diag_factor = jnp.linalg.cholesky(diag_block)  173 us
    psum x1, waiting for transfers between devices, from_root(): return lax.psum(jnp.where(mine, x, jnp.zeros_like(x)), axis)  86.3 us
    another operation x3, other arithmetic, per_device(): jax.scipy.linalg.solve_triangular(diag_factor, panel_columns.T, lower=True)  83.9 us
    all_gather x1, blocking collectives, per_device(): lax.all_gather(col_piece, 'row', axis=0, tiled=True)  35.1 us
    another operation x15, matrix products, per_device(): jax.scipy.linalg.solve_triangular(diag_factor, panel_columns.T, lower=True)  29.7 us
    dot_general x16, matrix products, orbit_kernel(): jnp.einsum('nf,mf->nm', row_feats, rolled, preferred_element_type=jnp.flo...  26.9 us
    all_to_all x1, blocking collectives, per_device(): lax.all_to_all(local_tile, 'row', split_axis=0, concat_axis=0, tiled=True)  23.3 us
  transfers between devices with their start and end apart: 3, of which 2 were waited for; matrix products, arithmetic and copies ran while one was open for 41% of the time, Pallas kernels for 0%

commit v1 on v0

v1 whole, which is shorter than its diff:
```python
import functools
import math

import jax
import jax.numpy as jnp
import numpy as np
from jax import lax
from jax.experimental import pallas as pl
from jax.experimental.pallas import tpu as pltpu
from jax.sharding import PartitionSpec as P

MESH = pl.DeviceIdType.MESH
f32 = jnp.float32
bf16 = jnp.bfloat16

ROTS = 16
SHARPNESS = 2.0
RIDGE = 0.1
F = 512
E = 640
G = 8
Q = 16
LOG2E = math.log2(math.e)
SCALE = 2.0 * LOG2E / F
VMEM = pl.BlockSpec(memory_space=pltpu.VMEM)
ROOM = 56 * 2**20


def split3(x):
    a = x.astype(bf16)
    x = x - a.astype(f32)
    b = x.astype(bf16)
    return a, b, (x - b.astype(f32)).astype(bf16)


def split(x):
    hi = x.astype(bf16)
    return hi, (x - hi.astype(f32)).astype(bf16)


def dot(a, b, dims):
    return lax.dot_general(a, b, (dims, ((), ())), preferred_element_type=f32)


def dot3(a, b, dims):
    ah, al = a
    bh, bl = b
    return dot(ah, bh, dims) + (dot(ah, bl, dims) + dot(al, bh, dims))


NT = ((1,), (1,))
NN = ((1,), (0,))
TN = ((0,), (0,))


def bin_table():
    angle = 2.0 * np.pi * np.arange(ROTS) / ROTS
    table = np.zeros((128, 128), np.float64)
    root = math.sqrt(SHARPNESS * LOG2E)
    for first, values in ((6, root * np.cos(angle)), (12, root * np.sin(angle))):
        parts, rest = [], values
        for _ in range(3):
            part = rest.astype(np.float32).astype(jnp.bfloat16).astype(np.float64)
            parts.append(part)
            rest = rest - part
        for lane, (left, right) in enumerate(((0, 0), (0, 1), (1, 0), (0, 2), (1, 1), (2, 0))):
            table[:ROTS, first + lane] = parts[left]
            table[:ROTS, 64 + first + lane] = parts[right]
    table[:ROTS, 3:6] = 1.0
    table[:ROTS, 64:67] = 1.0
    return table.astype(np.float32).astype(jnp.bfloat16)


def prep_kernel(pool_ref, ids_ref, rot_ref, table_ref, out_ref):
    def chunk(i, _):
        o = pl.multiple_of(i * 256, 256)
        n = pool_ref.shape[0]
        pick = lax.broadcasted_iota(jnp.int32, (256, n), 1) == ids_ref[pl.ds(o, 256), :]
        feats = dot(jnp.where(pick, 1.0, 0.0).astype(bf16), pool_ref[...], NN)
        norm = jnp.sum(feats * feats, axis=1, keepdims=True)
        a = jnp.broadcast_to(norm * (-LOG2E / F) - (SHARPNESS * LOG2E / 2.0 + 2.0), (256, 128))
        lane = lax.broadcasted_iota(jnp.int32, (256, 128), 1)
        bins = jnp.where(lane == rot_ref[pl.ds(o, 256), :], 1.0, 0.0).astype(bf16)
        extra = dot(bins, table_ref[...], NN)
        for k, part in enumerate(split3(a)):
            extra = jnp.where((lane == k) | (lane == 64 + 3 + k), part.astype(f32), extra)
        out_ref[pl.ds(o, 256), :F] = feats.astype(bf16)
        out_ref[pl.ds(o, 256), F:] = extra.astype(bf16)
        return 0

    lax.fori_loop(0, pool_ref.shape[0] // 256, chunk, 0)


def prep(pool, ids, rot):
    n = pool.shape[0]
    return pl.pallas_call(
        prep_kernel,
        out_shape=jax.ShapeDtypeStruct((n, E), bf16),
        in_specs=[VMEM] * 4,
        out_specs=VMEM,
        compiler_params=pltpu.CompilerParams(vmem_limit_bytes=ROOM),
    )(pool, ids.reshape(n, 1), rot.reshape(n, 1), jnp.asarray(bin_table()))


def exchange_kernel(ext_ref, rows_ref, cols_ref, lead_ref, local, s_row, r_row, s_col, r_col, s_lead, r_lead):
    p = lax.axis_index("row")
    q = lax.axis_index("col")
    barrier = pltpu.get_barrier_semaphore()
    for d in range(1, G):
        pl.semaphore_signal(barrier, inc=1, device_id=(lax.rem(p + d, G), q), device_id_type=MESH)
    for d in range(1, Q):
        pl.semaphore_signal(barrier, inc=1, device_id=(p, lax.rem(q + d, Q)), device_id_type=MESH)
    pl.semaphore_wait(barrier, G - 1 + Q - 1)

    def mine(k, width):
        return pl.ds(pl.multiple_of(k * width, width), width)

    def col_copy(d):
        return pltpu.make_async_remote_copy(
            src_ref=ext_ref.at[mine(q, 64), :],
            dst_ref=cols_ref.at[mine(p, 64), :],
            send_sem=s_col.at[d - 1], recv_sem=r_col.at[p],
            device_id=(lax.rem(p + d, G), q), device_id_type=MESH)

    def row_copy(d):
        other = lax.rem(p + d, G)
        return pltpu.make_async_remote_copy(
            src_ref=ext_ref.at[mine(other, 128), :],
            dst_ref=rows_ref.at[mine(p, 128), :],
            send_sem=s_row.at[d - 1], recv_sem=r_row.at[p],
            device_id=(other, q), device_id_type=MESH)

    def lead_copy(d):
        return pltpu.make_async_remote_copy(
            src_ref=cols_ref.at[pl.ds(0, 64), :],
            dst_ref=lead_ref.at[mine(q, 64), :],
            send_sem=s_lead.at[d - 1], recv_sem=r_lead.at[q],
            device_id=(p, lax.rem(q + d, Q)), device_id_type=MESH)

    def landed(ref, k, width, sem):
        return pltpu.make_async_remote_copy(
            src_ref=ref.at[mine(k, width), :], dst_ref=ref.at[mine(k, width), :],
            send_sem=s_row.at[0], recv_sem=sem.at[k],
            device_id=(lax.rem(p + 1, G), q), device_id_type=MESH)

    own_col = pltpu.make_async_copy(ext_ref.at[mine(q, 64), :], cols_ref.at[mine(p, 64), :], local.at[0])
    own_row = pltpu.make_async_copy(ext_ref.at[mine(p, 128), :], rows_ref.at[mine(p, 128), :], local.at[1])
    own_col.start()
    cols = [col_copy(d) for d in range(1, G)]
    for c in cols:
        c.start()
    own_row.start()
    own_col.wait()

    @pl.when(p != 0)
    def _():
        landed(cols_ref, 0, 64, r_col).wait_recv()

    own_lead = pltpu.make_async_copy(cols_ref.at[pl.ds(0, 64), :], lead_ref.at[mine(q, 64), :], local.at[2])
    own_lead.start()
    leads = [lead_copy(d) for d in range(1, Q)]
    for c in leads:
        c.start()
    rows = [row_copy(d) for d in range(1, G)]
    for c in rows:
        c.start()
    own_row.wait()
    own_lead.wait()
    for c in cols + leads + rows:
        c.wait_send()
    for k in range(1, G):
        @pl.when(p != k)
        def _():
            landed(cols_ref, k, 64, r_col).wait_recv()
    for k in range(Q):
        @pl.when(q != k)
        def _():
            landed(lead_ref, k, 64, r_lead).wait_recv()
    for k in range(G):
        @pl.when(p != k)
        def _():
            landed(rows_ref, k, 128, r_row).wait_recv()


def exchange(ext):
    n = ext.shape[0]
    dma = pltpu.SemaphoreType.DMA
    return pl.pallas_call(
        exchange_kernel,
        out_shape=(jax.ShapeDtypeStruct((n, E), bf16), jax.ShapeDtypeStruct((n // 2, E), bf16),
                   jax.ShapeDtypeStruct((n, E), bf16)),
        in_specs=[VMEM],
        out_specs=(VMEM,) * 3,
        scratch_shapes=[dma((3,)), dma((G - 1,)), dma((G,)), dma((G - 1,)), dma((G,)), dma((Q - 1,)), dma((Q,))],
        compiler_params=pltpu.CompilerParams(collective_id=0, has_side_effects=True, vmem_limit_bytes=ROOM),
    )(ext)


def turned(cols_ref, o, r4, aux):
    feats = cols_ref[pl.ds(o, 256), :F].astype(f32)
    for r in range(4):
        r4[r] = (jnp.roll(feats, 32 * r, axis=1) if r else feats).astype(bf16)
    aux[...] = jnp.roll(cols_ref[pl.ds(o, 256), F:].astype(f32), 64, axis=1).astype(bf16)


def tile(rows, r4, aux):
    lane = lax.broadcasted_iota(jnp.int32, (rows.shape[0], 128), 1)
    left = jnp.where(lane < 64, rows[:, F:].astype(f32), 0.0).astype(bf16)
    lhs = rows[:, :F]
    total = None
    for r in range(4):
        x = r4[r]
        for h in range(4):
            w = jnp.concatenate([x[:, 128 * ((k - h) % 4):128 * ((k - h) % 4) + 128] for k in range(4)], axis=1)
            e = jnp.exp2(dot(lhs, w, NT) * SCALE)
            total = e if total is None else total + e
    return total * jnp.exp2(dot(left, aux[...], NT))


def kernel_kernel(rows_ref, cols_ref, lead_ref, krh, krl, kch, kcl, ktr, lead_k, r4, aux):
    p = lax.axis_index("row")
    q = lax.axis_index("col")
    tm = 512

    def iotas(m, o, oc):
        return (o + lax.broadcasted_iota(jnp.int32, (m, 256), 0), oc + lax.broadcasted_iota(jnp.int32, (m, 256), 1))

    def lead_tile(n, _):
        oc = pl.multiple_of(n * 256, 256)
        turned(lead_ref, oc, r4, aux)

        def own(m, _):
            o = pl.multiple_of(m * 256, 256)
            k = tile(lead_ref[pl.ds(o, 256), :], r4, aux)
            i, j = iotas(256, o, oc)
            lead_k[pl.ds(o, 256), pl.ds(oc, 256)] = k + jnp.where(i == j, RIDGE, 0.0)
            return 0

        lax.fori_loop(0, n + 1, own, 0)

        def rows(m, _):
            o = pl.multiple_of(m * tm, tm)
            k = tile(rows_ref[pl.ds(o, tm), :], r4, aux)
            i, j = iotas(tm, o, oc)
            k = k + jnp.where((i < 128) & (i + p * 128 == j), RIDGE, 0.0)
            krh[pl.ds(o, tm), pl.ds(oc, 256)], krl[pl.ds(o, tm), pl.ds(oc, 256)] = split(k)
            return 0

        lax.fori_loop(0, rows_ref.shape[0] // tm, rows, 0)
        k = tile(cols_ref[...], r4, aux)
        kch[:, pl.ds(oc, 256)], kcl[:, pl.ds(oc, 256)] = split(k)
        return 0

    lax.fori_loop(0, lead_ref.shape[0] // 256, lead_tile, 0)

    def tr_tile(n, _):
        oc = pl.multiple_of(n * 256, 256)
        turned(cols_ref, oc, r4, aux)

        def rows(m, _):
            o = pl.multiple_of(m * tm, tm)
            k = tile(rows_ref[pl.ds(o, tm), :], r4, aux)
            i, j = iotas(tm, o, oc)
            same = ((i >> 7) == (j >> 6)) & (p * 128 + (i & 127) == q * 64 + (j & 63))
            k = k + jnp.where(same, RIDGE, 0.0)
            ktr[pl.ds(o, tm), pl.ds(oc, 256)] = jnp.where(j < 64, 0.0, k)
            return 0

        lax.fori_loop(0, rows_ref.shape[0] // tm, rows, 0)
        return 0

    lax.fori_loop(0, cols_ref.shape[0] // 256, tr_tile, 0)


def kernels(rows, cols, lead):
    n, c, w = rows.shape[0], cols.shape[0], lead.shape[0]
    s = jax.ShapeDtypeStruct
    return pl.pallas_call(
        kernel_kernel,
        out_shape=(s((n, w), bf16), s((n, w), bf16), s((c, w), bf16), s((c, w), bf16), s((n, c), f32), s((w, w), f32)),
        in_specs=[VMEM] * 3,
        out_specs=(VMEM,) * 6,
        scratch_shapes=[pltpu.VMEM((4, 256, F), bf16), pltpu.VMEM((256, 128), bf16)],
        compiler_params=pltpu.CompilerParams(vmem_limit_bytes=ROOM),
    )(rows, cols, lead)


def factor_block(S,V):
    sub=lax.broadcasted_iota(jnp.int32,(8,128),0)
    out=[]
    for b in range(16):
        R=S[b]; W=V[b]
        B=[jnp.broadcast_to(R[:,8*b+k:8*b+k+1],(8,128)) for k in range(8)]
        X=jnp.zeros((8,128),f32)
        for k in range(8):
            piv=jnp.broadcast_to(B[k][k:k+1,:],(8,128))
            rp=1.0/piv
            rs=lax.rsqrt(piv)
            here=sub==k
            mul=B[k]
            def step(Y):
                row=jnp.broadcast_to(Y[k:k+1,:],(8,128))*rp
                return jnp.where(here,row,Y-mul*row)
            X=jnp.where(here,W*rs,X)
            R=step(R); W=step(W)
            for j in range(k+1,8):
                B[j]=step(B[j])
        out.append(X)
        Rk=[jnp.broadcast_to(R[k:k+1,:],(8,128)) for k in range(8)]
        Wk=[jnp.broadcast_to(W[k:k+1,:],(8,128)) for k in range(8)]
        for r in range(b+1,16):
            c=[jnp.broadcast_to(S[r][:,8*b+k:8*b+k+1],(8,128)) for k in range(8)]
            S[r]=S[r]-(((c[0]*Rk[0]+c[1]*Rk[1])+(c[2]*Rk[2]+c[3]*Rk[3]))+((c[4]*Rk[4]+c[5]*Rk[5])+(c[6]*Rk[6]+c[7]*Rk[7])))
            V[r]=V[r]-(((c[0]*Wk[0]+c[1]*Wk[1])+(c[2]*Wk[2]+c[3]*Wk[3]))+((c[4]*Wk[4]+c[5]*Wk[5])+(c[6]*Wk[6]+c[7]*Wk[7])))
    return out

def chol_kernel(n, a_ref, x_ref, ph, plo):
    nb=n//128
    x_ref[...]=a_ref[...]
    ri=lax.broadcasted_iota(jnp.int32,(128,128),0); ci=lax.broadcasted_iota(jnp.int32,(128,128),1)
    eye=jnp.where(ri==ci,1.0,0.0).astype(f32)
    def outer(j,_):
        o=pl.multiple_of(j*128,128)
        D=x_ref[pl.ds(o,128),pl.ds(o,128)]
        S=[D[8*b:8*b+8] for b in range(16)]
        V=[eye[8*b:8*b+8] for b in range(16)]
        rows=factor_block(S,V)
        X=jnp.concatenate(rows,axis=0)
        x_ref[pl.ds(o,128),pl.ds(o,128)]=eye
        Xs=split(X)
        P=dot3(Xs,split(x_ref[pl.ds(o,128),:]),NN)
        x_ref[pl.ds(o,128),:]=P
        h,l=split(P)
        ph[...]=h; plo[...]=l
        def upd(i,_):
            oi=pl.multiple_of(i*128,128)
            F=(ph[:,pl.ds(oi,128)],plo[:,pl.ds(oi,128)])
            x_ref[pl.ds(oi,128),pl.ds(o,128)]=jnp.zeros((128,128),f32)
            x_ref[pl.ds(oi,128),:]=x_ref[pl.ds(oi,128),:]-dot3(F,(ph[...],plo[...]),TN)
            return 0
        lax.fori_loop(j+1,nb,upd,0)
        return 0
    lax.fori_loop(0,nb,outer,0)
    for j in range(nb-1):
        x_ref[j*128:(j+1)*128,(j+1)*128:]=jnp.zeros((128,n-(j+1)*128),f32)


def chol_inv(a):
    n = a.shape[0]
    return pl.pallas_call(
        functools.partial(chol_kernel, n),
        out_shape=jax.ShapeDtypeStruct((n, n), f32),
        in_specs=[VMEM],
        out_specs=VMEM,
        scratch_shapes=[pltpu.VMEM((128, n), bf16), pltpu.VMEM((128, n), bf16)],
        compiler_params=pltpu.CompilerParams(vmem_limit_bytes=ROOM),
    )(a)


def tail_kernel(krh, krl, kch, kcl, ktr, x_ref, out, xh, xl, ph, plo, zh, zl):
    q = lax.axis_index("col")
    n = x_ref.shape[0]
    for j in range(0, n, 256):
        xh[j:j + 256, :], xl[j:j + 256, :] = split(x_ref[j:j + 256, :])

    def cols(m, _):
        o = pl.ds(pl.multiple_of(m * 256, 256), 256)
        for j in range(0, n, 256):
            w = j + 256
            v = dot3((kch[o, :w], kcl[o, :w]), (xh[j:w, :w], xl[j:w, :w]), NT)
            ph[o, j:w], plo[o, j:w] = split(v)
        for j in range(0, n, 256):
            w = j + 256
            v = dot3((ph[o, j:], plo[o, j:]), (xh[j:, j:w], xl[j:, j:w]), NN)
            zh[o, j:w], zl[o, j:w] = split(v)
        return 0

    lax.fori_loop(0, kch.shape[0] // 256, cols, 0)
    first = pl.ds(pl.multiple_of(q * 64, 64), 64)
    zh[:64, :] = -xh[first, :]
    zl[:64, :] = -xl[first, :]

    def rows(m, _):
        o = pl.ds(pl.multiple_of(m * 256, 256), 256)
        out[o, :] = ktr[o, :] - dot3((krh[o, :], krl[o, :]), (zh[...], zl[...]), NT)
        return 0

    lax.fori_loop(0, krh.shape[0] // 256, rows, 0)


def tail(krh, krl, kch, kcl, ktr, x):
    n, w = krh.shape
    c = kch.shape[0]
    v = pltpu.VMEM
    return pl.pallas_call(
        tail_kernel,
        out_shape=jax.ShapeDtypeStruct((n, c), f32),
        in_specs=[VMEM] * 6,
        out_specs=VMEM,
        scratch_shapes=[v((w, w), bf16), v((w, w), bf16), v((c, w), bf16), v((c, w), bf16), v((c, w), bf16), v((c, w), bf16)],
        compiler_params=pltpu.CompilerParams(vmem_limit_bytes=ROOM),
    )(krh, krl, kch, kcl, ktr, x)


def per_device(pool, ids, rot):
    ext = prep(pool, ids, rot)
    rows, cols, lead = exchange(ext)
    krh, krl, kch, kcl, ktr, lead_k = kernels(rows, cols, lead)
    return tail(krh, krl, kch, kcl, ktr, chol_inv(lead_k))


def solution(mesh):
    return jax.shard_map(
        per_device,
        mesh=mesh,
        in_specs=(P("row", None), P("row", None), P("row")),
        out_specs=P("row", "col"),
        check_vma=False,
    )
```

time: 820 us -> 193 us (0.24)
  waiting for transfers between devices: 288 us -> 0 us
  other arithmetic: 271 us -> 0 us
  Pallas kernels: 0 us -> 190 us
  matrix products: 88.3 us -> 0 us
  local copies, waits for them, and re-layouts: 76.5 us -> 3.39 us
  blocking collectives: 69.1 us -> 0 us
  between operations: 19.7 us -> 0.01 us
    another operation x34 -> x0, other arithmetic: 257 us -> none  [the longest x31 173 us: per_device(): diag_factor = jnp.linalg.cholesky(diag_block)]
    all_gather x2 -> x0, waiting for transfers between devices: 202 us -> none  [the longest x1 202 us: per_device(): lax.all_gather(kernel_tile[None, :block_rows, :block_cols], ('row', 'col'...]
    pallas_call x0 -> x5, Pallas kernels: none -> 190 us  [the longest x1 61.9 us: kernels(): pl.pallas_call(kernel_kernel, out_shape=(s((n, w), bf16), s((n, w), bf16)...]
    psum x1 -> x0, waiting for transfers between devices: 86.3 us -> none  [from_root(): return lax.psum(jnp.where(mine, x, jnp.zeros_like(x)), axis)]
    another operation x29 -> x0, matrix products: 52.8 us -> none  [the longest x15 29.7 us: per_device(): jax.scipy.linalg.solve_triangular(diag_factor, panel_columns.T, lower=True)]
    dot_general x17 -> x0, matrix products: 35.5 us -> none  [the longest x16 26.9 us: orbit_kernel(): jnp.einsum('nf,mf->nm', row_feats, rolled, preferred_element_type=jnp.flo...]
    all_gather x1 -> x0, blocking collectives: 35.1 us -> none  [per_device(): lax.all_gather(col_piece, 'row', axis=0, tiled=True)]
    another operation x33 -> x0, local copies, waits for them, and re-layouts: 25.8 us -> none
  transfers between devices with their start and end apart: 3 -> 0, of which waited for: 2 -> 0; matrix products, arithmetic and copies ran while one was open for 41% -> 0% of each run, Pallas kernels for 0% -> 0%
where the time goes in v1:
time: 193 us
  Pallas kernels  190 us (98%)
  local copies, waits for them, and re-layouts  3.39 us (2%)
    pallas_call x1, Pallas kernels, kernels(): pl.pallas_call(kernel_kernel, out_shape=(s((n, w), bf16), s((n, w), bf16)...  61.9 us
    pallas_call x1, Pallas kernels, chol_inv(): pl.pallas_call(functools.partial(chol_kernel, n), out_shape=jax.ShapeDtyp...  56.7 us
    pallas_call x1, Pallas kernels, exchange(): pl.pallas_call(exchange_kernel, out_shape=(jax.ShapeDtypeStruct((n, E), b...  50.4 us
    pallas_call x1, Pallas kernels, tail(): pl.pallas_call(tail_kernel, out_shape=jax.ShapeDtypeStruct((n, c), f32),...  15.6 us
    pallas_call x1, Pallas kernels, prep(): pl.pallas_call(prep_kernel, out_shape=jax.ShapeDtypeStruct((n, E), bf16),...  4.99 us

profile of v1, /device:TPU:102, one launch (start us, length us, event | category | flops | bytes accessed | tf_op | source)
XLA Modules:
  0.0 193.0 jit_solution(3163749487782130550)
XLA Ops:
  0.0 1.7 copy.5.ids_ref
  1.7 1.7 copy.6.rot_ref
  3.4 5.0 %shard_map.46.ext_ref = bf16[1024,640]{1,0:T(8,128)(2,1)} custom-call(bf16[1024,512]{1,0:T(8,128)(2,1)} %pool_ref.1, s32[1024,1]{1,0:T(8,128)} %copy.5.ids_ref, s32[1024,1]{1,0:T(8,128)} %copy.6.rot_ref, bf16[128,128]{1,0:T(8,128)(2,1)} %constant.2.clone.table_ref), custom_call_target="tpu_custom_call" | custom-call | tf_op jit(solution)/shard_map/pallas_call | solution.py:96
  8.4 50.4 %shard_map.47 = (bf16[1024,640]{1,0:T(8,128)(2,1)}, bf16[512,640]{1,0:T(8,128)(2,1)}, bf16[1024,640]{1,0:T(8,128)(2,1)}) custom-call(bf16[1024,640]{1,0:T(8,128)(2,1)} %shard_map.46.ext_ref), custom_call_target="tpu_custom_call" | custom-call | tf_op jit(solution)/shard_map/pallas_call | solution.py:188
  58.8 61.9 %shard_map.48 = (bf16[1024,1024]{1,0:T(8,128)(2,1)}, bf16[1024,1024]{1,0:T(8,128)(2,1)}, bf16[512,1024]{1,0:T(8,128)(2,1)}, bf16[512,1024]{1,0:T(8,128)(2,1)}, f...) custom-call(bf16[1024,640]{1,0:T(8,128)(2,1)} %get-tuple-element.14.rows_ref, bf16[512,640]{1,0:T(8,128)(2,1)} %get-tuple-element.15.cols_ref, ...), custom_call_target="tpu_custom_call" | custom-call | tf_op jit(solution)/shard_map/pallas_call | solution.py:278
  120.7 56.7 %shard_map.49.x_ref = f32[1024,1024]{1,0:T(8,128)} custom-call(f32[1024,1024]{1,0:T(8,128)} %get-tuple-element.22.a_ref), custom_call_target="tpu_custom_call" | custom-call | tf_op jit(solution)/shard_map/pallas_call | solution.py:350
  177.4 15.6 %shard_map.50 = f32[1024,512]{1,0:T(8,128)} custom-call(bf16[1024,1024]{1,0:T(8,128)(2,1)} %get-tuple-element.17.krh, bf16[1024,1024]{1,0:T(8,128)(2,1)} %get-tuple-element.18.krl, bf16[512,1024]{1,0:T(8,128)(2,1)} %get-tuple-element.19.kch, bf16[512,1024]{1,0:T(8,128)(2,1)} %get-tuple-element.20.kcl, f32[1024,512]{1,0:T(8,128)} %get-tuple-element.21.ktr, ...), custom_call_target="tpu_custom_call" | custom-call | tf_op jit(solution)/shard_map/pallas_call | solution.py:395

commit v2 on v1

v2 whole, which is shorter than its diff:
```python
import functools
import math

import jax
import jax.numpy as jnp
import numpy as np
from jax import lax
from jax.experimental import pallas as pl
from jax.experimental.pallas import tpu as pltpu
from jax.sharding import PartitionSpec as P

MESH = pl.DeviceIdType.MESH
f32 = jnp.float32
bf16 = jnp.bfloat16

ROTS = 16
SHARPNESS = 2.0
RIDGE = 0.1
F = 512
E = 640
G = 8
Q = 16
LOG2E = math.log2(math.e)
SCALE = 2.0 * LOG2E / F
VMEM = pl.BlockSpec(memory_space=pltpu.VMEM)
ROOM = 56 * 2**20


def split3(x):
    a = x.astype(bf16)
    x = x - a.astype(f32)
    b = x.astype(bf16)
    return a, b, (x - b.astype(f32)).astype(bf16)


def split(x):
    hi = x.astype(bf16)
    return hi, (x - hi.astype(f32)).astype(bf16)


def dot(a, b, dims):
    return lax.dot_general(a, b, (dims, ((), ())), preferred_element_type=f32)


def dot3(a, b, dims):
    ah, al = a
    bh, bl = b
    return dot(ah, bh, dims) + (dot(ah, bl, dims) + dot(al, bh, dims))


NT = ((1,), (1,))
NN = ((1,), (0,))
TN = ((0,), (0,))


def bin_table():
    angle = 2.0 * np.pi * np.arange(ROTS) / ROTS
    table = np.zeros((128, 128), np.float64)
    root = math.sqrt(SHARPNESS * LOG2E)
    for first, values in ((6, root * np.cos(angle)), (12, root * np.sin(angle))):
        parts, rest = [], values
        for _ in range(3):
            part = rest.astype(np.float32).astype(jnp.bfloat16).astype(np.float64)
            parts.append(part)
            rest = rest - part
        for lane, (left, right) in enumerate(((0, 0), (0, 1), (1, 0), (0, 2), (1, 1), (2, 0))):
            table[:ROTS, first + lane] = parts[left]
            table[:ROTS, 64 + first + lane] = parts[right]
    table[:ROTS, 3:6] = 1.0
    table[:ROTS, 64:67] = 1.0
    return table.astype(np.float32).astype(jnp.bfloat16)


def prep_kernel(pool_ref, ids_ref, rot_ref, table_ref, out_ref):
    def chunk(i, _):
        o = pl.multiple_of(i * 256, 256)
        n = pool_ref.shape[0]
        pick = lax.broadcasted_iota(jnp.int32, (256, n), 1) == ids_ref[pl.ds(o, 256), :]
        feats = dot(jnp.where(pick, 1.0, 0.0).astype(bf16), pool_ref[...], NN)
        norm = jnp.sum(feats * feats, axis=1, keepdims=True)
        a = jnp.broadcast_to(norm * (-LOG2E / F) - (SHARPNESS * LOG2E / 2.0 + 2.0), (256, 128))
        lane = lax.broadcasted_iota(jnp.int32, (256, 128), 1)
        bins = jnp.where(lane == rot_ref[pl.ds(o, 256), :], 1.0, 0.0).astype(bf16)
        extra = dot(bins, table_ref[...], NN)
        for k, part in enumerate(split3(a)):
            extra = jnp.where((lane == k) | (lane == 64 + 3 + k), part.astype(f32), extra)
        out_ref[pl.ds(o, 256), :F] = feats.astype(bf16)
        out_ref[pl.ds(o, 256), F:] = extra.astype(bf16)
        return 0

    lax.fori_loop(0, pool_ref.shape[0] // 256, chunk, 0)


def prep(pool, ids, rot):
    n = pool.shape[0]
    return pl.pallas_call(
        prep_kernel,
        out_shape=jax.ShapeDtypeStruct((n, E), bf16),
        in_specs=[VMEM] * 4,
        out_specs=VMEM,
        compiler_params=pltpu.CompilerParams(vmem_limit_bytes=ROOM),
    )(pool, ids.reshape(n, 1), rot.reshape(n, 1), jnp.asarray(bin_table()))


def exchange_kernel(ext_ref, rows_ref, cols_ref, lead_ref, local, s_row, r_row, s_col, r_col, s_lead, r_lead):
    p = lax.axis_index("row")
    q = lax.axis_index("col")
    barrier = pltpu.get_barrier_semaphore()
    for d in range(1, G):
        pl.semaphore_signal(barrier, inc=1, device_id=(lax.rem(p + d, G), q), device_id_type=MESH)
    for d in range(1, Q):
        pl.semaphore_signal(barrier, inc=1, device_id=(p, lax.rem(q + d, Q)), device_id_type=MESH)
    pl.semaphore_wait(barrier, G - 1 + Q - 1)

    def mine(k, width):
        return pl.ds(pl.multiple_of(k * width, width), width)

    def col_copy(d):
        return pltpu.make_async_remote_copy(
            src_ref=ext_ref.at[mine(q, 64), :],
            dst_ref=cols_ref.at[mine(p, 64), :],
            send_sem=s_col.at[d - 1], recv_sem=r_col.at[p],
            device_id=(lax.rem(p + d, G), q), device_id_type=MESH)

    def row_copy(d):
        other = lax.rem(p + d, G)
        return pltpu.make_async_remote_copy(
            src_ref=ext_ref.at[mine(other, 128), :],
            dst_ref=rows_ref.at[mine(p, 128), :],
            send_sem=s_row.at[d - 1], recv_sem=r_row.at[p],
            device_id=(other, q), device_id_type=MESH)

    def lead_copy(d):
        return pltpu.make_async_remote_copy(
            src_ref=cols_ref.at[pl.ds(0, 64), :],
            dst_ref=lead_ref.at[mine(q, 64), :],
            send_sem=s_lead.at[d - 1], recv_sem=r_lead.at[q],
            device_id=(p, lax.rem(q + d, Q)), device_id_type=MESH)

    def landed(ref, k, width, sem):
        return pltpu.make_async_remote_copy(
            src_ref=ref.at[mine(k, width), :], dst_ref=ref.at[mine(k, width), :],
            send_sem=s_row.at[0], recv_sem=sem.at[k],
            device_id=(lax.rem(p + 1, G), q), device_id_type=MESH)

    own_col = pltpu.make_async_copy(ext_ref.at[mine(q, 64), :], cols_ref.at[mine(p, 64), :], local.at[0])
    own_row = pltpu.make_async_copy(ext_ref.at[mine(p, 128), :], rows_ref.at[mine(p, 128), :], local.at[1])
    own_col.start()
    cols = [col_copy(d) for d in range(1, G)]
    for c in cols:
        c.start()
    own_row.start()
    own_col.wait()

    @pl.when(p != 0)
    def _():
        landed(cols_ref, 0, 64, r_col).wait_recv()

    own_lead = pltpu.make_async_copy(cols_ref.at[pl.ds(0, 64), :], lead_ref.at[mine(q, 64), :], local.at[2])
    own_lead.start()
    leads = [lead_copy(d) for d in range(1, Q)]
    for c in leads:
        c.start()
    rows = [row_copy(d) for d in range(1, G)]
    for c in rows:
        c.start()
    own_row.wait()
    own_lead.wait()
    for c in cols + leads + rows:
        c.wait_send()
    for k in range(1, G):
        @pl.when(p != k)
        def _():
            landed(cols_ref, k, 64, r_col).wait_recv()
    for k in range(Q):
        @pl.when(q != k)
        def _():
            landed(lead_ref, k, 64, r_lead).wait_recv()
    for k in range(G):
        @pl.when(p != k)
        def _():
            landed(rows_ref, k, 128, r_row).wait_recv()


def exchange(ext):
    n = ext.shape[0]
    dma = pltpu.SemaphoreType.DMA
    return pl.pallas_call(
        exchange_kernel,
        out_shape=(jax.ShapeDtypeStruct((n, E), bf16), jax.ShapeDtypeStruct((n // 2, E), bf16),
                   jax.ShapeDtypeStruct((n, E), bf16)),
        in_specs=[VMEM],
        out_specs=(VMEM,) * 3,
        scratch_shapes=[dma((3,)), dma((G - 1,)), dma((G,)), dma((G - 1,)), dma((G,)), dma((Q - 1,)), dma((Q,))],
        compiler_params=pltpu.CompilerParams(collective_id=0, has_side_effects=True, vmem_limit_bytes=ROOM),
    )(ext)


def roll_into(src, o, r4):
    feats = src[pl.ds(o, 256), :F].astype(f32)
    for r in range(4):
        r4[r, pl.ds(o, 256), :] = (jnp.roll(feats, 32 * r, axis=1) if r else feats).astype(bf16)


def tile(rows, rolled, right):
    lane = lax.broadcasted_iota(jnp.int32, (rows.shape[0], 128), 1)
    left = jnp.where(lane < 64, rows[:, F:].astype(f32), 0.0).astype(bf16)
    lhs = rows[:, :F]
    total = None
    for r in range(4):
        x = rolled(r)
        for h in range(4):
            w = jnp.concatenate([x[:, 128 * ((k - h) % 4):128 * ((k - h) % 4) + 128] for k in range(4)], axis=1)
            e = jnp.exp2(dot(lhs, w, NT) * SCALE)
            total = e if total is None else total + e
    return total * jnp.exp2(dot(left, right, NT))


def lead_kernel(lead_ref, r4, lead_k):
    n = lead_ref.shape[0]

    def columns(c, _):
        o = pl.multiple_of(c * 256, 256)
        cols = pl.ds(o, 256)
        roll_into(lead_ref, o, r4)
        right = jnp.roll(lead_ref[cols, F:].astype(f32), 64, axis=1).astype(bf16)

        def above(m, _):
            rows = pl.ds(pl.multiple_of(m * 256, 256), 256)
            k = tile(lead_ref[rows, :], lambda r: r4[r, cols, :], right)
            i = m * 256 + lax.broadcasted_iota(jnp.int32, (256, 256), 0)
            j = o + lax.broadcasted_iota(jnp.int32, (256, 256), 1)
            k = k + jnp.where(i == j, RIDGE, 0.0)
            lead_k[rows, cols] = k
            lead_k[cols, rows] = k.T
            return 0

        lax.fori_loop(0, c + 1, above, 0)
        return 0

    lax.fori_loop(0, n // 256, columns, 0)


def lead_block(lead):
    n = lead.shape[0]
    return pl.pallas_call(
        lead_kernel,
        out_shape=(jax.ShapeDtypeStruct((4, n, F), bf16), jax.ShapeDtypeStruct((n, n), f32)),
        in_specs=[VMEM],
        out_specs=(VMEM, VMEM),
        compiler_params=pltpu.CompilerParams(vmem_limit_bytes=ROOM),
    )(lead)


def sub_row(y, k):
    return jnp.broadcast_to(y[k:k + 1, :], (8, 128))


def lane_col(y, k):
    return jnp.broadcast_to(y[:, k:k + 1], (8, 128))


def tree(terms):
    while len(terms) > 1:
        terms = [terms[i] + terms[i + 1] for i in range(0, len(terms), 2)]
    return terms[0]


def factor_steps(d, out):
    sub = lax.broadcasted_iota(jnp.int32, (8, 128), 0)
    lane = lax.broadcasted_iota(jnp.int32, (8, 128), 1)
    s = [d[8 * b:8 * b + 8] for b in range(16)]
    v = [jnp.where(lane == sub + 8 * b, 1.0, 0.0).astype(f32) for b in range(16)]
    for b in range(16):
        r, w = s[b], v[b]
        cols = [lane_col(r, 8 * b + k) for k in range(8)]
        x = jnp.zeros((8, 128), f32)
        for k in range(0, 8, 2):
            p11, p12, p22 = sub_row(cols[k], k), sub_row(cols[k + 1], k), sub_row(cols[k + 1], k + 1)
            det = p11 * p22 - p12 * p12
            rd = 1.0 / det
            m1 = jnp.where(sub == k, -1.0, jnp.where(sub == k + 1, 0.0, cols[k]))
            m2 = jnp.where(sub == k, 0.0, jnp.where(sub == k + 1, -1.0, cols[k + 1]))
            pair = (sub == k) | (sub == k + 1)

            def step(y):
                y1, y2 = sub_row(y, k), sub_row(y, k + 1)
                z1 = (p22 * y1 - p12 * y2) * rd
                z2 = (p11 * y2 - p12 * y1) * rd
                return (jnp.where(pair, 0.0, y) - m1 * z1) - m2 * z2, z2

            x = jnp.where(sub == k, w * lax.rsqrt(p11), x)
            r, _ = step(r)
            w, z = step(w)
            x = jnp.where(sub == k + 1, z * (det * lax.rsqrt(det * p11)), x)
            for j in range(k + 2, 8):
                cols[j], _ = step(cols[j])
            yield
        out.append(x)
        rk = [sub_row(r, k) for k in range(8)]
        wk = [sub_row(w, k) for k in range(8)]
        for i in range(b + 1, 16):
            c = [lane_col(s[i], 8 * b + k) for k in range(8)]
            s[i] = s[i] - tree([c[k] * rk[k] for k in range(8)])
            v[i] = v[i] - tree([c[k] * wk[k] for k in range(8)])


def main_kernel(rows_ref, cols_ref, lead_ref, r4, lead_k, out, c_ref, xh, xl, bh, bl, dref, r4c, aux, krh, krl, kch,
                kcl, ktr, acc, ph, plo, zh, zl):
    p = lax.axis_index("row")
    q = lax.axis_index("col")
    n = lead_ref.shape[0]
    for c in range(n // 256):
        aux[c * 256:c * 256 + 256, :] = jnp.roll(
            lead_ref[c * 256:c * 256 + 256, F:].astype(f32), 64, axis=1).astype(bf16)
    for c in range(cols_ref.shape[0] // 256):
        roll_into(cols_ref, c * 256, r4c)
        aux[n + c * 256:n + c * 256 + 256, :] = jnp.roll(
            cols_ref[c * 256:c * 256 + 256, F:].astype(f32), 64, axis=1).astype(bf16)
    c_ref[:256, :] = jnp.zeros((256, n), f32)
    c_ref[256:, :] = lead_k[...]
    bh[...] = jnp.zeros_like(bh)
    bl[...] = jnp.zeros_like(bl)
    dref[...] = lead_k[:256, :256]
    ri = lax.broadcasted_iota(jnp.int32, (256, 256), 0)
    ci = lax.broadcasted_iota(jnp.int32, (256, 256), 1)
    eye = jnp.where(ri == ci, 1.0, 0.0).astype(f32)

    def blk(k):
        return pl.ds(pl.multiple_of(k * 256, 256), 256)

    def cs(k):
        return pl.ds(k * 256, 256)

    def k_tile(t, left_ref, lo, rolled, ro, auxo, store):
        lhs = left_ref[lo, :F]
        for r in range(4):
            for h in range(4):
                x = rolled[r, ro, :]
                w = jnp.concatenate([x[:, 128 * ((k - h) % 4):128 * ((k - h) % 4) + 128] for k in range(4)], axis=1)
                e = jnp.exp2(dot(lhs, w, NT) * SCALE)
                if r + h == 0:
                    acc[t] = e
                else:
                    acc[t] = acc[t] + e
                yield
        lane = lax.broadcasted_iota(jnp.int32, (256, 128), 1)
        left = jnp.where(lane < 64, left_ref[lo, F:].astype(f32), 0.0).astype(bf16)
        store(acc[t] * jnp.exp2(dot(left, aux[auxo, :], NT)))
        yield

    def solve_row(g, prev):
        x = (bh[...], bl[...])
        for c in range(4):
            r = jnp.where(jnp.int32(c) == g - 1, eye, c_ref[blk(g), cs(c)])
            xh[blk(g), cs(c)], xl[blk(g), cs(c)] = split(dot3(x, split(r), NN))
            yield

    def update(g, prev):
        for r in range(3):
            i = lax.rem(g + r, 4)
            keep = jnp.where(r < 4 - g, 1.0, 0.0).astype(f32)
            f = split(dot3(split(c_ref[blk(i + 1), blk(prev)] * keep), (bh[...], bl[...]), NT))
            yield
            for c in range(4):
                old = jnp.where(jnp.int32(c) == g - 1, 0.0, c_ref[blk(i + 1), cs(c)])
                c_ref[blk(i + 1), cs(c)] = old - dot3(f, (xh[blk(g), cs(c)], xl[blk(g), cs(c)]), NN)
                yield

    def outer(g, _):
        prev = jnp.maximum(g - 1, 0)
        nxt = jnp.minimum(g + 1, 3)

        def work():
            yield from solve_row(g, prev)
            yield from update(g, prev)
            for m in range(4):
                def store(k, m=m):
                    k = k + jnp.where((ri + m * 256 < 128) & (ri + (m * 256 + p * 128) == ci + g * 256), RIDGE, 0.0)
                    krh[cs(m), blk(g)], krl[cs(m), blk(g)] = split(k)

                yield from k_tile(m % 2, rows_ref, cs(m), r4, blk(g), blk(g), store)
            for m in range(2):
                def store(k, m=m):
                    kch[cs(m), blk(g)], kcl[cs(m), blk(g)] = split(k)

                yield from k_tile(m % 2, cols_ref, cs(m), r4, blk(g), blk(g), store)
            for c in range(2):
                def store(k, c=c):
                    i, j = ri + g * 256, ci + c * 256
                    same = ((i >> 7) == (j >> 6)) & (p * 128 + (i & 127) == q * 64 + (j & 63))
                    k = k + jnp.where(same, RIDGE, 0.0)
                    ktr[blk(g), cs(c)] = jnp.where(j < 64, 0.0, k)

                yield from k_tile(c % 2, rows_ref, blk(g), r4c, cs(c), cs(4 + c), store)

        todo = work()
        credit = [0.0]

        def fill(amount):
            credit[0] += amount
            while credit[0] >= 1.0:
                credit[0] -= 1.0
                next(todo, None)

        per = 148.0 / 128.0
        d00 = dref[:128, :128]
        d10 = dref[128:, :128]
        d11 = dref[128:, 128:]
        out0, out1 = [], []
        for _s in factor_steps(d00, out0):
            fill(per)
        x0 = jnp.concatenate(out0, axis=0)
        x0s = split(x0)
        l10 = split(dot3(split(d10), x0s, NT))
        fill(2)
        d11 = d11 - dot3(l10, l10, NT)
        fill(2)
        g10 = split(dot3(l10, x0s, NN))
        for _s in factor_steps(d11, out1):
            fill(per)
        for _s in todo:
            pass
        x1 = jnp.concatenate(out1, axis=0)
        x10 = -dot3(split(x1), g10, NN)
        bh[:128, :128], bl[:128, :128] = x0s
        bh[128:, :128], bl[128:, :128] = split(x10)
        bh[128:, 128:], bl[128:, 128:] = split(x1)
        f = split(dot3(split(c_ref[blk(nxt + 1), blk(g)]), (bh[...], bl[...]), NT))
        dref[...] = c_ref[blk(nxt + 1), blk(nxt)] - dot3(f, f, NT)
        return 0

    lax.fori_loop(0, 4, outer, 0)
    for _s in solve_row(4, 3):
        pass

    def pcols(m, _):
        o = pl.ds(pl.multiple_of(m * 256, 256), 256)
        for j in range(0, n, 256):
            w = j + 256
            a = dot3((kch[o, :w], kcl[o, :w]), (xh[j + 256:w + 256, :w], xl[j + 256:w + 256, :w]), NT)
            ph[o, j:w], plo[o, j:w] = split(a)
        for j in range(0, n, 256):
            w = j + 256
            a = dot3((ph[o, j:], plo[o, j:]), (xh[j + 256:, j:w], xl[j + 256:, j:w]), NN)
            zh[o, j:w], zl[o, j:w] = split(a)
        return 0

    lax.fori_loop(0, cols_ref.shape[0] // 256, pcols, 0)
    first = pl.ds(pl.multiple_of(q * 64 + 256, 64), 64)
    keep = lax.broadcasted_iota(jnp.int32, (64, n), 1) <= q * 64 + lax.broadcasted_iota(jnp.int32, (64, n), 0)
    zh[:64, :] = jnp.where(keep, -xh[first, :].astype(f32), 0.0).astype(bf16)
    zl[:64, :] = jnp.where(keep, -xl[first, :].astype(f32), 0.0).astype(bf16)

    def last(m, _):
        o = pl.ds(pl.multiple_of(m * 256, 256), 256)
        out[o, :] = ktr[o, :] - dot3((krh[o, :], krl[o, :]), (zh[...], zl[...]), NT)
        return 0

    lax.fori_loop(0, rows_ref.shape[0] // 256, last, 0)


def main(rows, cols, lead, r4, lead_k):
    n, c, w = rows.shape[0], cols.shape[0], lead.shape[0]
    v = pltpu.VMEM
    return pl.pallas_call(
        main_kernel,
        out_shape=jax.ShapeDtypeStruct((n, c), f32),
        in_specs=[VMEM] * 5,
        out_specs=VMEM,
        scratch_shapes=[
            v((w + 256, w), f32), v((w + 256, w), bf16), v((w + 256, w), bf16), v((256, 256), bf16),
            v((256, 256), bf16), v((256, 256), f32), v((4, c, F), bf16), v((w + c, 128), bf16),
            v((n, w), bf16), v((n, w), bf16), v((c, w), bf16), v((c, w), bf16), v((n, c), f32), v((2, 256, 256), f32),
            v((c, w), bf16), v((c, w), bf16), v((c, w), bf16), v((c, w), bf16),
        ],
        compiler_params=pltpu.CompilerParams(vmem_limit_bytes=ROOM),
    )(rows, cols, lead, r4, lead_k)


def per_device(pool, ids, rot):
    ext = prep(pool, ids, rot)
    rows, cols, lead = exchange(ext)
    r4, lead_k = lead_block(lead)
    return main(rows, cols, lead, r4, lead_k)


def solution(mesh):
    return jax.shard_map(
        per_device,
        mesh=mesh,
        in_specs=(P("row", None), P("row", None), P("row")),
        out_specs=P("row", "col"),
        check_vma=False,
    )
```

time: 193 us -> 154 us (0.80)
  Pallas kernels: 190 us -> 150 us
    pallas_call x3 -> x2, Pallas kernels: 134 us -> 94.5 us  [the longest x1 74.3 us: main(): pl.pallas_call(main_kernel, out_shape=jax.ShapeDtypeStruct((n, c), f32),...]
where the time goes in v2:
time: 154 us; the launch traced here: 153 us
  Pallas kernels  150 us (97%)
  local copies, waits for them, and re-layouts  3.39 us (2%)
    pallas_call x1, Pallas kernels, main(): pl.pallas_call(main_kernel, out_shape=jax.ShapeDtypeStruct((n, c), f32),...  74.3 us
    pallas_call x1, Pallas kernels, exchange(): pl.pallas_call(exchange_kernel, out_shape=(jax.ShapeDtypeStruct((n, E), b...  50.4 us
    pallas_call x1, Pallas kernels, lead_block(): pl.pallas_call(lead_kernel, out_shape=(jax.ShapeDtypeStruct((4, n, F), bf...  20.1 us
    pallas_call x1, Pallas kernels, prep(): pl.pallas_call(prep_kernel, out_shape=jax.ShapeDtypeStruct((n, E), bf16),...  4.99 us

profile of v2, /device:TPU:102, one launch (start us, length us, event | category | flops | bytes accessed | tf_op | source)
XLA Modules:
  0.0 153.3 jit_solution(11962377259981180209)
XLA Ops:
  0.0 1.7 %copy.5.ids_ref = s32[1024,1]{1,0:T(8,128)} copy(s32[1024,1]{0,1:T(1,128)} %bitcast.2) | data formatting | bytes 8192 | tf_op jit(solution)/shard_map/reshape | solution.py:102
  1.7 1.7 %copy.6.rot_ref = s32[1024,1]{1,0:T(8,128)} copy(s32[1024,1]{0,1:T(1,128)} %bitcast.3) | data formatting | bytes 8192 | tf_op jit(solution)/shard_map/reshape | solution.py:102
  3.4 5.0 %shard_map.46.ext_ref = bf16[1024,640]{1,0:T(8,128)(2,1)} custom-call(bf16[1024,512]{1,0:T(8,128)(2,1)} %pool_ref.1, s32[1024,1]{1,0:T(8,128)} %copy.5.ids_ref, s32[1024,1]{1,0:T(8,128)} %copy.6.rot_ref, bf16[128,128]{1,0:T(8,128)(2,1)} %constant.2.clone.table_ref), custom_call_target="tpu_custom_call" | custom-call | tf_op jit(solution)/shard_map/pallas_call | solution.py:96
  8.4 50.4 %shard_map.47 = (bf16[1024,640]{1,0:T(8,128)(2,1)}, bf16[512,640]{1,0:T(8,128)(2,1)}, bf16[1024,640]{1,0:T(8,128)(2,1)}) custom-call(bf16[1024,640]{1,0:T(8,128)(2,1)} %shard_map.46.ext_ref), custom_call_target="tpu_custom_call" | custom-call | tf_op jit(solution)/shard_map/pallas_call | solution.py:188
  58.8 20.1 %shard_map.48 = (bf16[4,1024,512]{2,1,0:T(8,128)(2,1)}, f32[1024,1024]{1,0:T(8,128)}) custom-call(bf16[1024,640]{1,0:T(8,128)(2,1)} %get-tuple-element.12.lead_ref), custom_call_target="tpu_custom_call" | custom-call | tf_op jit(solution)/shard_map/pallas_call | solution.py:246
  79.0 74.3 %shard_map.49 = f32[1024,512]{1,0:T(8,128)} custom-call(bf16[1024,640]{1,0:T(8,128)(2,1)} %get-tuple-element.10.rows_ref, bf16[512,640]{1,0:T(8,128)(2,1)} %get-tuple-element.11.cols_ref, bf16[1024,640]{1,0:T(8,128)(2,1)} %get-tuple-element.12.lead_ref, bf16[4,1024,512]{2,1,0:T(8,128)(2,1)} %get-tuple-element.13.r4, f32[1024,1024]{1,0:T(8,128)} %get-tuple-element.14.lead_k), custom_call_target="tpu_custom_call" | custom-call | tf_op jit(solution)/shard_map/pallas_call | solution.py:466

commit v3 on v2

--- a/solution.py
+++ b/solution.py
@@ -71,135 +71,14 @@
     return table.astype(np.float32).astype(jnp.bfloat16)
 
 
-def prep_kernel(pool_ref, ids_ref, rot_ref, table_ref, out_ref):
-    def chunk(i, _):
-        o = pl.multiple_of(i * 256, 256)
-        n = pool_ref.shape[0]
-        pick = lax.broadcasted_iota(jnp.int32, (256, n), 1) == ids_ref[pl.ds(o, 256), :]
-        feats = dot(jnp.where(pick, 1.0, 0.0).astype(bf16), pool_ref[...], NN)
-        norm = jnp.sum(feats * feats, axis=1, keepdims=True)
-        a = jnp.broadcast_to(norm * (-LOG2E / F) - (SHARPNESS * LOG2E / 2.0 + 2.0), (256, 128))
-        lane = lax.broadcasted_iota(jnp.int32, (256, 128), 1)
-        bins = jnp.where(lane == rot_ref[pl.ds(o, 256), :], 1.0, 0.0).astype(bf16)
-        extra = dot(bins, table_ref[...], NN)
-        for k, part in enumerate(split3(a)):
-            extra = jnp.where((lane == k) | (lane == 64 + 3 + k), part.astype(f32), extra)
-        out_ref[pl.ds(o, 256), :F] = feats.astype(bf16)
-        out_ref[pl.ds(o, 256), F:] = extra.astype(bf16)
-        return 0
-
-    lax.fori_loop(0, pool_ref.shape[0] // 256, chunk, 0)
-
-
-def prep(pool, ids, rot):
-    n = pool.shape[0]
-    return pl.pallas_call(
-        prep_kernel,
-        out_shape=jax.ShapeDtypeStruct((n, E), bf16),
-        in_specs=[VMEM] * 4,
-        out_specs=VMEM,
-        compiler_params=pltpu.CompilerParams(vmem_limit_bytes=ROOM),
-    )(pool, ids.reshape(n, 1), rot.reshape(n, 1), jnp.asarray(bin_table()))
-
-
-def exchange_kernel(ext_ref, rows_ref, cols_ref, lead_ref, local, s_row, r_row, s_col, r_col, s_lead, r_lead):
-    p = lax.axis_index("row")
-    q = lax.axis_index("col")
-    barrier = pltpu.get_barrier_semaphore()
-    for d in range(1, G):
-        pl.semaphore_signal(barrier, inc=1, device_id=(lax.rem(p + d, G), q), device_id_type=MESH)
-    for d in range(1, Q):
-        pl.semaphore_signal(barrier, inc=1, device_id=(p, lax.rem(q + d, Q)), device_id_type=MESH)
-    pl.semaphore_wait(barrier, G - 1 + Q - 1)
-
-    def mine(k, width):
-        return pl.ds(pl.multiple_of(k * width, width), width)
-
-    def col_copy(d):
-        return pltpu.make_async_remote_copy(
-            src_ref=ext_ref.at[mine(q, 64), :],
-            dst_ref=cols_ref.at[mine(p, 64), :],
-            send_sem=s_col.at[d - 1], recv_sem=r_col.at[p],
-            device_id=(lax.rem(p + d, G), q), device_id_type=MESH)
-
-    def row_copy(d):
-        other = lax.rem(p + d, G)
-        return pltpu.make_async_remote_copy(
-            src_ref=ext_ref.at[mine(other, 128), :],
-            dst_ref=rows_ref.at[mine(p, 128), :],
-            send_sem=s_row.at[d - 1], recv_sem=r_row.at[p],
-            device_id=(other, q), device_id_type=MESH)
-
-    def lead_copy(d):
-        return pltpu.make_async_remote_copy(
-            src_ref=cols_ref.at[pl.ds(0, 64), :],
-            dst_ref=lead_ref.at[mine(q, 64), :],
-            send_sem=s_lead.at[d - 1], recv_sem=r_lead.at[q],
-            device_id=(p, lax.rem(q + d, Q)), device_id_type=MESH)
-
-    def landed(ref, k, width, sem):
-        return pltpu.make_async_remote_copy(
-            src_ref=ref.at[mine(k, width), :], dst_ref=ref.at[mine(k, width), :],
-            send_sem=s_row.at[0], recv_sem=sem.at[k],
-            device_id=(lax.rem(p + 1, G), q), device_id_type=MESH)
-
-    own_col = pltpu.make_async_copy(ext_ref.at[mine(q, 64), :], cols_ref.at[mine(p, 64), :], local.at[0])
-    own_row = pltpu.make_async_copy(ext_ref.at[mine(p, 128), :], rows_ref.at[mine(p, 128), :], local.at[1])
-    own_col.start()
-    cols = [col_copy(d) for d in range(1, G)]
-    for c in cols:
-        c.start()
-    own_row.start()
-    own_col.wait()
-
-    @pl.when(p != 0)
-    def _():
-        landed(cols_ref, 0, 64, r_col).wait_recv()
-
-    own_lead = pltpu.make_async_copy(cols_ref.at[pl.ds(0, 64), :], lead_ref.at[mine(q, 64), :], local.at[2])
-    own_lead.start()
-    leads = [lead_copy(d) for d in range(1, Q)]
-    for c in leads:
-        c.start()
-    rows = [row_copy(d) for d in range(1, G)]
-    for c in rows:
-        c.start()
-    own_row.wait()
-    own_lead.wait()
-    for c in cols + leads + rows:
-        c.wait_send()
-    for k in range(1, G):
-        @pl.when(p != k)
-        def _():
-            landed(cols_ref, k, 64, r_col).wait_recv()
-    for k in range(Q):
-        @pl.when(q != k)
-        def _():
-            landed(lead_ref, k, 64, r_lead).wait_recv()
-    for k in range(G):
-        @pl.when(p != k)
-        def _():
-            landed(rows_ref, k, 128, r_row).wait_recv()
-
-
-def exchange(ext):
-    n = ext.shape[0]
-    dma = pltpu.SemaphoreType.DMA
-    return pl.pallas_call(
-        exchange_kernel,
-        out_shape=(jax.ShapeDtypeStruct((n, E), bf16), jax.ShapeDtypeStruct((n // 2, E), bf16),
-                   jax.ShapeDtypeStruct((n, E), bf16)),
-        in_specs=[VMEM],
-        out_specs=(VMEM,) * 3,
-        scratch_shapes=[dma((3,)), dma((G - 1,)), dma((G,)), dma((G - 1,)), dma((G,)), dma((Q - 1,)), dma((Q,))],
-        compiler_params=pltpu.CompilerParams(collective_id=0, has_side_effects=True, vmem_limit_bytes=ROOM),
-    )(ext)
-
-
 def roll_into(src, o, r4):
     feats = src[pl.ds(o, 256), :F].astype(f32)
     for r in range(4):
         r4[r, pl.ds(o, 256), :] = (jnp.roll(feats, 32 * r, axis=1) if r else feats).astype(bf16)
+
+
+def right_lanes(src, o):
+    return jnp.roll(src[pl.ds(o, 256), F:].astype(f32), 64, axis=1).astype(bf16)
 
 
 def tile(rows, rolled, right):
@@ -216,40 +95,201 @@
     return total * jnp.exp2(dot(left, right, NT))
 
 
-def lead_kernel(lead_ref, r4, lead_k):
-    n = lead_ref.shape[0]
-
-    def columns(c, _):
+def exchange_kernel(pool_ref, ids_ref, rot_ref, table_ref, rows_ref, cols_ref, r4, aux, lead_k, ext_ref, lead_ref,
+                    local, s_col, r_first, r_col, s_lead, r_lead, s_leadf, r_leadf, s_row, r_row, s_rowf, r_rowf,
+                    s_tile, r_tile):
+    p = lax.axis_index("row")
+    q = lax.axis_index("col")
+    core = lax.rem(q, 2)
+    sibling = (p, q + 1 - 2 * core)
+    n = pool_ref.shape[0]
+    barrier = pltpu.get_barrier_semaphore()
+    rows_to = [(lax.rem(p + d, G), q) for d in range(1, G)]
+    cols_to = [(p, lax.rem(q + 2 * d, Q)) for d in range(1, Q // 2)]
+    for device in rows_to + cols_to + [sibling]:
+        pl.semaphore_signal(barrier, inc=1, device_id=device, device_id_type=MESH)
+
+    def features(k):
+        o = pl.ds(pl.multiple_of(k * 128, 128), 128)
+        lane = lax.broadcasted_iota(jnp.int32, (128, 128), 1)
+        down = jnp.broadcast_to(ids_ref[pl.ds(k, 1), :].astype(f32), (128, 128)).T.astype(jnp.int32)
+        bins = jnp.broadcast_to(rot_ref[pl.ds(k, 1), :].astype(f32), (128, 128)).T.astype(jnp.int32)
+        pick = jnp.concatenate(
+            [jnp.where(down == lane + c * 128, 1.0, 0.0).astype(bf16) for c in range(n // 128)], axis=1)
+        feats = dot(pick, pool_ref[...], NN)
+        norm = jnp.sum(feats * feats, axis=1, keepdims=True)
+        a = jnp.broadcast_to(norm * (-LOG2E / F) - (SHARPNESS * LOG2E / 2.0 + 2.0), (128, 128))
+        extra = dot(jnp.where(bins == lane, 1.0, 0.0).astype(bf16), table_ref[...], NN)
+        for i, part in enumerate(split3(a)):
+            extra = jnp.where((lane == i) | (lane == 64 + 3 + i), part.astype(f32), extra)
+        ext_ref[o, :F] = feats.astype(bf16)
+        ext_ref[o, F:] = extra.astype(bf16)
+
+    def piece(k):
+        return pl.ds(pl.multiple_of(k * 64, 64), 64)
+
+    def copy(src, dst, send, recv, device):
+        return pltpu.make_async_remote_copy(
+            src_ref=src, dst_ref=dst, send_sem=send, recv_sem=recv, device_id=device, device_id_type=MESH)
+
+    def arrived(ref, sem):
+        copy(ref, ref, s_col.at[0], sem, sibling).wait_recv()
+
+    first = lax.div(q, 2)
+    features(first)
+    pl.semaphore_wait(barrier, G - 1 + Q // 2)
+    own = piece(q)
+    starts = [copy(ext_ref.at[own, :], lead_ref.at[own, :], s_col.at[d - 1], r_first.at[0], rows_to[d - 1])
+              for d in range(1, G)]
+
+    @pl.when(p == 0)
+    def _():
+        for c in starts:
+            c.start()
+
+    def others(i, _):
+        features(lax.rem(first + i, n // 128))
+        return 0
+
+    lax.fori_loop(1, n // 128, others, 0)
+
+    @pl.when(p == 0)
+    def _():
+        c = pltpu.make_async_copy(ext_ref.at[own, :], lead_ref.at[own, :], local.at[0])
+        c.start()
+        c.wait()
+
+    @pl.when(p != 0)
+    def _():
+        arrived(lead_ref.at[own, :], r_first.at[0])
+
+    leads = [copy(lead_ref.at[own, :], lead_ref.at[own, :], s_lead.at[d], r_leadf.at[d] if d == 0 else r_lead.at[d - 1],
+                  sibling if d == 0 else cols_to[d - 1]) for d in range(Q // 2)]
+    for c in leads[1:] + leads[:1]:
+        c.start()
+    half = [copy(ext_ref.at[piece(2 * to[0] + core), :], rows_ref.at[piece(2 * p + core), :], s_row.at[d], r_row.at[d],
+                 to) for d, to in enumerate(rows_to)]
+    cols = [copy(ext_ref.at[own, :], cols_ref.at[piece(p), :], s_col.at[d], r_col.at[d], to)
+            for d, to in enumerate(rows_to)]
+    own_rows = pltpu.make_async_copy(
+        ext_ref.at[pl.ds(pl.multiple_of(p * 128, 128), 128), :], rows_ref.at[pl.ds(pl.multiple_of(p * 128, 128), 128), :],
+        local.at[1])
+    own_rows.start()
+    own_cols = pltpu.make_async_copy(lead_ref.at[own, :], cols_ref.at[piece(0), :], local.at[2])
+    own_cols.start()
+    own_piece = pltpu.make_async_copy(ext_ref.at[own, :], cols_ref.at[piece(p), :], local.at[0])
+
+    @pl.when(p != 0)
+    def _():
+        own_piece.start()
+
+    passed = []
+    for d in range(1, Q // 2):
+        at = lead_ref.at[piece(lax.rem(q - 2 * d + Q, Q)), :]
+        arrived(at, r_lead.at[d - 1])
+        c = copy(at, at, s_leadf.at[d - 1], r_leadf.at[d], sibling)
+        c.start()
+        passed.append(c)
+    for c in half:
+        c.start()
+
+    @pl.when(p != 0)
+    def _():
+        for c in cols:
+            c.start()
+
+    for d in range(Q // 2):
+        at = lead_ref.at[piece(lax.rem(sibling[1] - 2 * d + Q, Q)), :]
+        arrived(at, r_leadf.at[d])
+
+    def turn(c, _):
         o = pl.multiple_of(c * 256, 256)
-        cols = pl.ds(o, 256)
         roll_into(lead_ref, o, r4)
-        right = jnp.roll(lead_ref[cols, F:].astype(f32), 64, axis=1).astype(bf16)
-
-        def above(m, _):
-            rows = pl.ds(pl.multiple_of(m * 256, 256), 256)
-            k = tile(lead_ref[rows, :], lambda r: r4[r, cols, :], right)
-            i = m * 256 + lax.broadcasted_iota(jnp.int32, (256, 256), 0)
-            j = o + lax.broadcasted_iota(jnp.int32, (256, 256), 1)
-            k = k + jnp.where(i == j, RIDGE, 0.0)
-            lead_k[rows, cols] = k
-            lead_k[cols, rows] = k.T
-            return 0
-
-        lax.fori_loop(0, c + 1, above, 0)
+        aux[pl.ds(o, 256), :] = right_lanes(lead_ref, o)
         return 0
 
-    lax.fori_loop(0, n // 256, columns, 0)
-
-
-def lead_block(lead):
-    n = lead.shape[0]
+    lax.fori_loop(0, n // 256, turn, 0)
+
+    def blk(k):
+        return pl.ds(pl.multiple_of(k * 256, 256), 256)
+
+    def lead_tile(m, c):
+        k = tile(lead_ref[blk(m), :], lambda r: r4[r, blk(c), :], aux[blk(c), :])
+        i = m * 256 + lax.broadcasted_iota(jnp.int32, (256, 256), 0)
+        j = c * 256 + lax.broadcasted_iota(jnp.int32, (256, 256), 1)
+        return k + jnp.where(i == j, RIDGE, 0.0)
+
+    def swap(k, m, c):
+        at = lead_k.at[blk(m), blk(c)]
+        return copy(at, at, s_tile.at[k], r_tile.at[k], sibling)
+
+    def place(t, side):
+        above = (0, 0, 1)[t] + side * ((0, 1, 2)[t] - (0, 0, 1)[t])
+        right = (1, 2, 2)[t] + side * (3 - (1, 2, 2)[t])
+        return above, right
+
+    swaps, theirs = [], []
+    for t in range(2):
+        m = t + 2 * core
+        lead_k[blk(m), blk(m)] = lead_tile(m, m)
+        c = swap(t, m, m)
+        c.start()
+        swaps.append(c)
+        theirs.append((t, t + 2 * (1 - core), t + 2 * (1 - core)))
+    rowsf = []
+    for t in range(3):
+        m, c = place(t, core)
+        k = lead_tile(m, c)
+        lead_k[blk(m), blk(c)] = k
+        lead_k[blk(c), blk(m)] = k.T
+        for s, (a, b) in enumerate(((m, c), (c, m))):
+            w = swap(2 + 2 * t + s, a, b)
+            w.start()
+            swaps.append(w)
+        a, b = place(t, 1 - core)
+        theirs += [(2 + 2 * t, a, b), (3 + 2 * t, b, a)]
+        if t == 1:
+            for d in range(G - 1):
+                at = rows_ref.at[piece(2 * lax.rem(p - d - 1 + G, G) + core), :]
+                arrived(at, r_row.at[d])
+                w = copy(at, at, s_rowf.at[d], r_rowf.at[d], sibling)
+                w.start()
+                rowsf.append(w)
+    own_rows.wait()
+    own_cols.wait()
+
+    @pl.when(p != 0)
+    def _():
+        own_piece.wait()
+    for c in leads + passed + half + rowsf + swaps + cols:
+        c.wait_send()
+    for d in range(G - 1):
+        arrived(rows_ref.at[piece(2 * lax.rem(p - d - 1 + G, G) + 1 - core), :], r_rowf.at[d])
+        sender = lax.rem(p - d - 1 + G, G)
+
+        @pl.when(sender != 0)
+        def _():
+            arrived(cols_ref.at[piece(sender), :], r_col.at[d])
+    for k, m, c in theirs:
+        arrived(lead_k.at[blk(m), blk(c)], r_tile.at[k])
+
+
+def exchange(pool, ids, rot):
+    n = pool.shape[0]
+    dma = pltpu.SemaphoreType.DMA
+    s = jax.ShapeDtypeStruct
     return pl.pallas_call(
-        lead_kernel,
-        out_shape=(jax.ShapeDtypeStruct((4, n, F), bf16), jax.ShapeDtypeStruct((n, n), f32)),
-        in_specs=[VMEM],
-        out_specs=(VMEM, VMEM),
-        compiler_params=pltpu.CompilerParams(vmem_limit_bytes=ROOM),
-    )(lead)
+        exchange_kernel,
+        out_shape=(s((n, E), bf16), s((n // 2, E), bf16), s((4, n, F), bf16), s((n, 128), bf16), s((n, n), f32)),
+        in_specs=[VMEM] * 4,
+        out_specs=(VMEM,) * 5,
+        scratch_shapes=[
+            pltpu.VMEM((n, E), bf16), pltpu.VMEM((n, E), bf16), dma((3,)), dma((G - 1,)), dma((1,)), dma((G - 1,)),
+            dma((8,)), dma((7,)), dma((7,)), dma((8,)), dma((G - 1,)), dma((G - 1,)), dma((G - 1,)), dma((G - 1,)),
+            dma((8,)), dma((8,)),
+        ],
+        compiler_params=pltpu.CompilerParams(collective_id=0, has_side_effects=True, vmem_limit_bytes=ROOM),
+    )(pool, ids.reshape(n // 128, 128), rot.reshape(n // 128, 128), jnp.asarray(bin_table()))
 
 
 def sub_row(y, k):
@@ -305,18 +345,15 @@
             v[i] = v[i] - tree([c[k] * wk[k] for k in range(8)])
 
 
-def main_kernel(rows_ref, cols_ref, lead_ref, r4, lead_k, out, c_ref, xh, xl, bh, bl, dref, r4c, aux, krh, krl, kch,
+def main_kernel(rows_ref, cols_ref, r4, lead_aux, lead_k, out, c_ref, xh, xl, bh, bl, dref, r4c, aux, krh, krl, kch,
                 kcl, ktr, acc, ph, plo, zh, zl):
     p = lax.axis_index("row")
     q = lax.axis_index("col")
-    n = lead_ref.shape[0]
-    for c in range(n // 256):
-        aux[c * 256:c * 256 + 256, :] = jnp.roll(
-            lead_ref[c * 256:c * 256 + 256, F:].astype(f32), 64, axis=1).astype(bf16)
+    n = lead_k.shape[0]
+    aux[:n, :] = lead_aux[...]
     for c in range(cols_ref.shape[0] // 256):
         roll_into(cols_ref, c * 256, r4c)
-        aux[n + c * 256:n + c * 256 + 256, :] = jnp.roll(
-            cols_ref[c * 256:c * 256 + 256, F:].astype(f32), 64, axis=1).astype(bf16)
+        aux[n + c * 256:n + c * 256 + 256, :] = right_lanes(cols_ref, c * 256)
     c_ref[:256, :] = jnp.zeros((256, n), f32)
     c_ref[256:, :] = lead_k[...]
     bh[...] = jnp.zeros_like(bh)
@@ -460,8 +497,8 @@
     lax.fori_loop(0, rows_ref.shape[0] // 256, last, 0)
 
 
-def main(rows, cols, lead, r4, lead_k):
-    n, c, w = rows.shape[0], cols.shape[0], lead.shape[0]
+def main(rows, cols, r4, aux, lead_k):
+    n, c, w = rows.shape[0], cols.shape[0], lead_k.shape[0]
     v = pltpu.VMEM
     return pl.pallas_call(
         main_kernel,
@@ -475,14 +512,11 @@
             v((c, w), bf16), v((c, w), bf16), v((c, w), bf16), v((c, w), bf16),
         ],
         compiler_params=pltpu.CompilerParams(vmem_limit_bytes=ROOM),
-    )(rows, cols, lead, r4, lead_k)
+    )(rows, cols, r4, aux, lead_k)
 
 
 def per_device(pool, ids, rot):
-    ext = prep(pool, ids, rot)
-    rows, cols, lead = exchange(ext)
-    r4, lead_k = lead_block(lead)
-    return main(rows, cols, lead, r4, lead_k)
+    return main(*exchange(pool, ids, rot))
 
 
 def solution(mesh):

time: 154 us -> 126 us (0.82)
  Pallas kernels: 150 us -> 125 us
  local copies, waits for them, and re-layouts: 3.39 us -> 0 us
    pallas_call x3 -> x1, Pallas kernels: 75.6 us -> 50.6 us  [exchange(): pl.pallas_call(exchange_kernel, out_shape=(s((n, E), bf16), s((n // 2, E)...]
    reshape x2 -> x0, local copies, waits for them, and re-layouts: 3.39 us -> none  [the longest x1 1.7 us: prep(): rot.reshape(n, 1)]
where the time goes in v3:
time: 126 us; the launch traced here: 125 us
  Pallas kernels  125 us (99%)
    pallas_call x1, Pallas kernels, main(): pl.pallas_call(main_kernel, out_shape=jax.ShapeDtypeStruct((n, c), f32),...  74 us
    pallas_call x1, Pallas kernels, exchange(): pl.pallas_call(exchange_kernel, out_shape=(s((n, E), bf16), s((n // 2, E)...  50.6 us

profile of v3, /device:TPU:102, one launch (start us, length us, event | category | flops | bytes accessed | tf_op | source)
XLA Modules:
  0.0 124.6 jit_solution(11770186230756862559)
XLA Ops:
  0.0 50.6 %shard_map.46 = (bf16[1024,640]{1,0:T(8,128)(2,1)}, bf16[512,640]{1,0:T(8,128)(2,1)}, bf16[4,1024,512]{2,1,0:T(8,128)(2,1)}, bf16[1024,128]{1,0:T(8,128)(2,1)}, f32[1024,1024]{1,0:T(8,128)}) custom-call(bf16[1024,512]{1,0:T(8,128)(2,1)} %pool_ref.1, s32[8,128]{1,0:T(8,128)} %bitcast.2, s32[8,128]{1,0:T(8,128)} %bitcast.3, ...), custom_call_target="tpu_custom_call" | custom-call | tf_op jit(solution)/shard_map/pallas_call | solution.py:281
  50.6 74.0 %shard_map.47 = f32[1024,512]{1,0:T(8,128)} custom-call(bf16[1024,640]{1,0:T(8,128)(2,1)} %get-tuple-element.10.rows_ref, bf16[512,640]{1,0:T(8,128)(2,1)} %get-tuple-element.11.cols_ref, bf16[4,1024,512]{2,1,0:T(8,128)(2,1)} %get-tuple-element.12.r4, bf16[1024,128]{1,0:T(8,128)(2,1)} %get-tuple-element.13.lead_aux, f32[1024,1024]{1,0:T(8,128)} %get-tuple-element.14.lead_k), custom_call_target="tpu_custom_call" | custom-call | tf_op jit(solution)/shard_map/pallas_call | solution.py:503

commit v4 on v3

v4 whole, which is shorter than its diff:
```python
import functools
import math

import jax
import jax.numpy as jnp
import numpy as np
from jax import lax
from jax.experimental import pallas as pl
from jax.experimental.pallas import tpu as pltpu
from jax.sharding import PartitionSpec as P

MESH = pl.DeviceIdType.MESH
f32 = jnp.float32
bf16 = jnp.bfloat16

ROTS = 16
SHARPNESS = 2.0
RIDGE = 0.1
F = 512
E = 640
G = 8
Q = 16
LOG2E = math.log2(math.e)
SCALE = 2.0 * LOG2E / F
VMEM = pl.BlockSpec(memory_space=pltpu.VMEM)
ROOM = 56 * 2**20


def split3(x):
    a = x.astype(bf16)
    x = x - a.astype(f32)
    b = x.astype(bf16)
    return a, b, (x - b.astype(f32)).astype(bf16)


def split(x):
    hi = x.astype(bf16)
    return hi, (x - hi.astype(f32)).astype(bf16)


def dot(a, b, dims):
    return lax.dot_general(a, b, (dims, ((), ())), preferred_element_type=f32)


def dot3(a, b, dims):
    ah, al = a
    bh, bl = b
    return dot(ah, bh, dims) + (dot(ah, bl, dims) + dot(al, bh, dims))


NT = ((1,), (1,))
NN = ((1,), (0,))
TN = ((0,), (0,))


def bin_table():
    angle = 2.0 * np.pi * np.arange(ROTS) / ROTS
    table = np.zeros((128, 128), np.float64)
    root = math.sqrt(SHARPNESS * LOG2E)
    for first, values in ((6, root * np.cos(angle)), (12, root * np.sin(angle))):
        parts, rest = [], values
        for _ in range(3):
            part = rest.astype(np.float32).astype(jnp.bfloat16).astype(np.float64)
            parts.append(part)
            rest = rest - part
        for lane, (left, right) in enumerate(((0, 0), (0, 1), (1, 0), (0, 2), (1, 1), (2, 0))):
            table[:ROTS, first + lane] = parts[left]
            table[:ROTS, 64 + first + lane] = parts[right]
    table[:ROTS, 3:6] = 1.0
    table[:ROTS, 64:67] = 1.0
    return table.astype(np.float32).astype(jnp.bfloat16)


def roll_into(src, o, r4):
    feats = src[pl.ds(o, 256), :F].astype(f32)
    for r in range(4):
        r4[r, pl.ds(o, 256), :] = (jnp.roll(feats, 32 * r, axis=1) if r else feats).astype(bf16)


def right_lanes(src, o):
    return jnp.roll(src[pl.ds(o, 256), F:].astype(f32), 64, axis=1).astype(bf16)


def tile(rows, rolled, right):
    lane = lax.broadcasted_iota(jnp.int32, (rows.shape[0], 128), 1)
    left = jnp.where(lane < 64, rows[:, F:].astype(f32), 0.0).astype(bf16)
    lhs = rows[:, :F]
    total = None
    for r in range(4):
        x = rolled(r)
        for h in range(4):
            w = jnp.concatenate([x[:, 128 * ((k - h) % 4):128 * ((k - h) % 4) + 128] for k in range(4)], axis=1)
            e = jnp.exp2(dot(lhs, w, NT) * SCALE)
            total = e if total is None else total + e
    return total * jnp.exp2(dot(left, right, NT))


def sub_row(y, k):
    return jnp.broadcast_to(y[k:k + 1, :], (8, 128))


def lane_col(y, k):
    return jnp.broadcast_to(y[:, k:k + 1], (8, 128))


def tree(terms):
    while len(terms) > 1:
        terms = [terms[i] + terms[i + 1] for i in range(0, len(terms), 2)]
    return terms[0]


def factor_steps(d, out):
    sub = lax.broadcasted_iota(jnp.int32, (8, 128), 0)
    lane = lax.broadcasted_iota(jnp.int32, (8, 128), 1)
    s = [d[8 * b:8 * b + 8] for b in range(16)]
    v = [jnp.where(lane == sub + 8 * b, 1.0, 0.0).astype(f32) for b in range(16)]
    for b in range(16):
        r, w = s[b], v[b]
        cols = [lane_col(r, 8 * b + k) for k in range(8)]
        x = jnp.zeros((8, 128), f32)
        for k in range(0, 8, 2):
            p11, p12, p22 = sub_row(cols[k], k), sub_row(cols[k + 1], k), sub_row(cols[k + 1], k + 1)
            det = p11 * p22 - p12 * p12
            rd = 1.0 / det
            m1 = jnp.where(sub == k, -1.0, jnp.where(sub == k + 1, 0.0, cols[k]))
            m2 = jnp.where(sub == k, 0.0, jnp.where(sub == k + 1, -1.0, cols[k + 1]))
            pair = (sub == k) | (sub == k + 1)

            def step(y):
                y1, y2 = sub_row(y, k), sub_row(y, k + 1)
                z1 = (p22 * y1 - p12 * y2) * rd
                z2 = (p11 * y2 - p12 * y1) * rd
                return (jnp.where(pair, 0.0, y) - m1 * z1) - m2 * z2, z2

            x = jnp.where(sub == k, w * lax.rsqrt(p11), x)
            r, _ = step(r)
            w, z = step(w)
            x = jnp.where(sub == k + 1, z * (det * lax.rsqrt(det * p11)), x)
            for j in range(k + 2, 8):
                cols[j], _ = step(cols[j])
            yield
        out.append(x)
        rk = [sub_row(r, k) for k in range(8)]
        wk = [sub_row(w, k) for k in range(8)]
        for i in range(b + 1, 16):
            c = [lane_col(s[i], 8 * b + k) for k in range(8)]
            s[i] = s[i] - tree([c[k] * rk[k] for k in range(8)])
            v[i] = v[i] - tree([c[k] * wk[k] for k in range(8)])


def fused_kernel(pool_ref, ids_ref, rot_ref, table_ref, out, rows_ref, cols_ref, r4, aux, ext_ref, lead_ref, c_ref, xh,
                 xl, bh, bl, dref, r4c, krh, krl, kch, kcl, ktr, acc, ph, plo, zh, zl, local, s_col, r_first, r_col,
                 s_lead, r_lead, s_leadf, r_leadf, s_row, r_row, s_rowf, r_rowf, s_tile, r_tile, s_half, r_half):
    p = lax.axis_index("row")
    q = lax.axis_index("col")
    core = lax.rem(q, 2)
    sibling = (p, q + 1 - 2 * core)
    n = pool_ref.shape[0]
    barrier = pltpu.get_barrier_semaphore()
    rows_to = [(lax.rem(p + d, G), q) for d in range(1, G)]
    cols_to = [(p, lax.rem(q + 2 * d, Q)) for d in range(1, Q // 2)]
    for device in rows_to + cols_to + [sibling]:
        pl.semaphore_signal(barrier, inc=1, device_id=device, device_id_type=MESH)

    def features(k):
        o = pl.ds(pl.multiple_of(k * 128, 128), 128)
        lane = lax.broadcasted_iota(jnp.int32, (128, 128), 1)
        down = jnp.broadcast_to(ids_ref[pl.ds(k, 1), :].astype(f32), (128, 128)).T.astype(jnp.int32)
        bins = jnp.broadcast_to(rot_ref[pl.ds(k, 1), :].astype(f32), (128, 128)).T.astype(jnp.int32)
        pick = jnp.concatenate(
            [jnp.where(down == lane + c * 128, 1.0, 0.0).astype(bf16) for c in range(n // 128)], axis=1)
        feats = dot(pick, pool_ref[...], NN)
        norm = jnp.sum(feats * feats, axis=1, keepdims=True)
        a = jnp.broadcast_to(norm * (-LOG2E / F) - (SHARPNESS * LOG2E / 2.0 + 2.0), (128, 128))
        extra = dot(jnp.where(bins == lane, 1.0, 0.0).astype(bf16), table_ref[...], NN)
        for i, part in enumerate(split3(a)):
            extra = jnp.where((lane == i) | (lane == 64 + 3 + i), part.astype(f32), extra)
        ext_ref[o, :F] = feats.astype(bf16)
        ext_ref[o, F:] = extra.astype(bf16)

    def piece(k):
        return pl.ds(pl.multiple_of(k * 64, 64), 64)

    def copy(src, dst, send, recv, device):
        return pltpu.make_async_remote_copy(
            src_ref=src, dst_ref=dst, send_sem=send, recv_sem=recv, device_id=device, device_id_type=MESH)

    def arrived(ref, sem):
        copy(ref, ref, s_col.at[0], sem, sibling).wait_recv()

    first = lax.div(q, 2)
    features(first)
    pl.semaphore_wait(barrier, G - 1 + Q // 2)
    own = piece(q)
    starts = [copy(ext_ref.at[own, :], lead_ref.at[own, :], s_col.at[d - 1], r_first.at[0], rows_to[d - 1])
              for d in range(1, G)]

    @pl.when(p == 0)
    def _():
        for c in starts:
            c.start()

    def others(i, _):
        features(lax.rem(first + i, n // 128))
        return 0

    lax.fori_loop(1, n // 128, others, 0)

    half = [copy(ext_ref.at[piece(2 * to[0] + core), :], rows_ref.at[piece(2 * p + core), :], s_row.at[d], r_row.at[d],
                 to) for d, to in enumerate(rows_to)]
    cols = [copy(ext_ref.at[own, :], cols_ref.at[piece(p), :], s_col.at[d], r_col.at[d], to)
            for d, to in enumerate(rows_to)]
    for c in half:
        c.start()

    @pl.when(p != 0)
    def _():
        for c in cols:
            c.start()

    @pl.when(p == 0)
    def _():
        c = pltpu.make_async_copy(ext_ref.at[own, :], lead_ref.at[own, :], local.at[0])
        c.start()
        c.wait()

    @pl.when(p != 0)
    def _():
        arrived(lead_ref.at[own, :], r_first.at[0])

    leads = [copy(lead_ref.at[own, :], lead_ref.at[own, :], s_lead.at[d], r_leadf.at[d] if d == 0 else r_lead.at[d - 1],
                  sibling if d == 0 else cols_to[d - 1]) for d in range(Q // 2)]
    for c in leads[1:] + leads[:1]:
        c.start()
    own_rows = pltpu.make_async_copy(
        ext_ref.at[pl.ds(pl.multiple_of(p * 128, 128), 128), :], rows_ref.at[pl.ds(pl.multiple_of(p * 128, 128), 128), :],
        local.at[1])
    own_rows.start()
    own_cols = pltpu.make_async_copy(lead_ref.at[own, :], cols_ref.at[piece(0), :], local.at[2])
    own_cols.start()
    own_piece = pltpu.make_async_copy(ext_ref.at[own, :], cols_ref.at[piece(p), :], local.at[0])

    @pl.when(p != 0)
    def _():
        own_piece.start()

    passed = []
    for d in range(1, Q // 2):
        at = lead_ref.at[piece(lax.rem(q - 2 * d + Q, Q)), :]
        arrived(at, r_lead.at[d - 1])
        c = copy(at, at, s_leadf.at[d - 1], r_leadf.at[d], sibling)
        c.start()
        passed.append(c)
    for d in range(Q // 2):
        at = lead_ref.at[piece(lax.rem(sibling[1] - 2 * d + Q, Q)), :]
        arrived(at, r_leadf.at[d])

    def turn(c, _):
        o = pl.multiple_of(c * 256, 256)
        roll_into(lead_ref, o, r4)
        aux[pl.ds(o, 256), :] = right_lanes(lead_ref, o)
        return 0

    lax.fori_loop(0, n // 256, turn, 0)

    def blk(k):
        return pl.ds(pl.multiple_of(k * 256, 256), 256)

    def lead_tile(m, c):
        k = tile(lead_ref[blk(m), :], lambda r: r4[r, blk(c), :], aux[blk(c), :])
        i = m * 256 + lax.broadcasted_iota(jnp.int32, (256, 256), 0)
        j = c * 256 + lax.broadcasted_iota(jnp.int32, (256, 256), 1)
        return k + jnp.where(i == j, RIDGE, 0.0)

    def swap(k, m, c):
        at = c_ref.at[blk(m + 1), blk(c)]
        return copy(at, at, s_tile.at[k], r_tile.at[k], sibling)

    def place(t, side):
        above = (0, 0, 1)[t] + side * ((0, 1, 2)[t] - (0, 0, 1)[t])
        right = (1, 2, 2)[t] + side * (3 - (1, 2, 2)[t])
        return above, right

    swaps, theirs = [], []
    for t in range(2):
        m = t + 2 * core
        c_ref[blk(m + 1), blk(m)] = lead_tile(m, m)
        c = swap(t, m, m)
        c.start()
        swaps.append(c)
        theirs.append((t, t + 2 * (1 - core), t + 2 * (1 - core)))
    rowsf = []
    for t in range(3):
        m, c = place(t, core)
        k = lead_tile(m, c)
        c_ref[blk(m + 1), blk(c)] = k
        c_ref[blk(c + 1), blk(m)] = k.T
        for s, (a, b) in enumerate(((m, c), (c, m))):
            w = swap(2 + 2 * t + s, a, b)
            w.start()
            swaps.append(w)
        a, b = place(t, 1 - core)
        theirs += [(2 + 2 * t, a, b), (3 + 2 * t, b, a)]
        if t == 0:
            for d in range(G - 1):
                at = rows_ref.at[piece(2 * lax.rem(p - d - 1 + G, G) + core), :]
                arrived(at, r_row.at[d])
                w = copy(at, at, s_rowf.at[d], r_rowf.at[d], sibling)
                w.start()
                rowsf.append(w)
    own_rows.wait()
    own_cols.wait()

    @pl.when(p != 0)
    def _():
        own_piece.wait()
    for c in swaps:
        c.wait_send()
    for d in range(G - 1):
        arrived(rows_ref.at[piece(2 * lax.rem(p - d - 1 + G, G) + 1 - core), :], r_rowf.at[d])
        sender = lax.rem(p - d - 1 + G, G)

        @pl.when(sender != 0)
        def _():
            arrived(cols_ref.at[piece(sender), :], r_col.at[d])
    for k, m, c in theirs:
        arrived(c_ref.at[blk(m + 1), blk(c)], r_tile.at[k])

    c_ref[:256, :] = jnp.zeros((256, n), f32)
    bh[...] = jnp.zeros_like(bh)
    bl[...] = jnp.zeros_like(bl)
    kch[:64, :] = jnp.zeros((64, n), bf16)
    kcl[:64, :] = jnp.zeros((64, n), bf16)
    ri = lax.broadcasted_iota(jnp.int32, (256, 256), 0)
    ci = lax.broadcasted_iota(jnp.int32, (256, 256), 1)
    eye = jnp.where(ri == ci, 1.0, 0.0).astype(f32)
    for c in range(cols_ref.shape[0] // 256):
        roll_into(cols_ref, c * 256, r4c)
        aux[n + c * 256:n + c * 256 + 256, :] = right_lanes(cols_ref, c * 256)
    dref[...] = c_ref[256:512, :256]

    def cs(k):
        return pl.ds(k * 256, 256)

    def k_tile(t, left_ref, lo, rolled, ro, auxo, store):
        lhs = left_ref[lo, :F]
        wide = lhs.shape[0]
        for r in range(4):
            for h in range(4):
                x = rolled[r, ro, :]
                w = jnp.concatenate([x[:, 128 * ((k - h) % 4):128 * ((k - h) % 4) + 128] for k in range(4)], axis=1)
                e = jnp.exp2(dot(lhs, w, NT) * SCALE)
                if r + h == 0:
                    acc[t, :wide, :] = e
                else:
                    acc[t, :wide, :] = acc[t, :wide, :] + e
                yield
        lane = lax.broadcasted_iota(jnp.int32, (wide, 128), 1)
        left = jnp.where(lane < 64, left_ref[lo, F:].astype(f32), 0.0).astype(bf16)
        store(acc[t, :wide, :] * jnp.exp2(dot(left, aux[auxo, :], NT)))
        yield

    def solve_row(g, prev):
        x = (bh[...], bl[...])
        for c in range(4):
            r = jnp.where(jnp.int32(c) == g - 1, eye, c_ref[blk(g), cs(c)])
            xh[blk(g), cs(c)], xl[blk(g), cs(c)] = split(dot3(x, split(r), NN))
            yield

    def update(g, prev):
        for r in range(3):
            i = lax.rem(g + r, 4)
            keep = jnp.where(r < 4 - g, 1.0, 0.0).astype(f32)
            f = split(dot3(split(c_ref[blk(i + 1), blk(prev)] * keep), (bh[...], bl[...]), NT))
            yield
            for c in range(4):
                old = jnp.where(jnp.int32(c) == g - 1, 0.0, c_ref[blk(i + 1), cs(c)])
                c_ref[blk(i + 1), cs(c)] = old - dot3(f, (xh[blk(g), cs(c)], xl[blk(g), cs(c)]), NN)
                yield

    def outer(g, _):
        prev = jnp.maximum(g - 1, 0)
        nxt = jnp.minimum(g + 1, 3)

        def work():
            yield from solve_row(g, prev)
            yield from update(g, prev)
            for m in range(2):
                o = blk(2 * core + m)

                def store(k, m=m, o=o):
                    i = ri + (2 * core + m) * 256
                    k = k + jnp.where((i < 128) & (i + p * 128 == ci + g * 256), RIDGE, 0.0)
                    krh[o, blk(g)], krl[o, blk(g)] = split(k)

                yield from k_tile(m % 2, rows_ref, o, r4, blk(g), blk(g), store)
            for m in range(2):
                o = pl.ds(64 + 224 * m, 224)

                def store(k, o=o):
                    kch[o, blk(g)], kcl[o, blk(g)] = split(k)

                yield from k_tile(m % 2, cols_ref, o, r4, blk(g), blk(g), store)
            for c in range(2):
                def store(k, c=c):
                    i, j = ri + g * 256, ci + c * 256
                    same = ((i >> 7) == (j >> 6)) & (p * 128 + (i & 127) == q * 64 + (j & 63))
                    k = k + jnp.where(same, RIDGE, 0.0)
                    ktr[blk(g), cs(c)] = jnp.where(j < 64, 0.0, k)

                yield from k_tile(c % 2, rows_ref, blk(g), r4c, cs(c), cs(4 + c), store)

        todo = work()
        credit = [0.0]

        def fill(amount):
            credit[0] += amount
            while credit[0] >= 1.0:
                credit[0] -= 1.0
                next(todo, None)

        per = 114.0 / 128.0
        d00 = dref[:128, :128]
        d10 = dref[128:, :128]
        d11 = dref[128:, 128:]
        out0, out1 = [], []
        for _s in factor_steps(d00, out0):
            fill(per)
        x0 = jnp.concatenate(out0, axis=0)
        x0s = split(x0)
        l10 = split(dot3(split(d10), x0s, NT))
        fill(2)
        d11 = d11 - dot3(l10, l10, NT)
        fill(2)
        g10 = split(dot3(l10, x0s, NN))
        for _s in factor_steps(d11, out1):
            fill(per)
        for _s in todo:
            pass
        x1 = jnp.concatenate(out1, axis=0)
        x10 = -dot3(split(x1), g10, NN)
        bh[:128, :128], bl[:128, :128] = x0s
        bh[128:, :128], bl[128:, :128] = split(x10)
        bh[128:, 128:], bl[128:, 128:] = split(x1)
        f = split(dot3(split(c_ref[blk(nxt + 1), blk(g)]), (bh[...], bl[...]), NT))
        dref[...] = c_ref[blk(nxt + 1), blk(nxt)] - dot3(f, f, NT)
        for c in halves(g, core):
            c.start()
        return 0

    def halves(g, side):
        refs = [(krh, 0), (krl, 1), (krh, 2), (krl, 3)]
        return [copy(ref.at[blk(2 * side + k // 2), blk(g)], ref.at[blk(2 * side + k // 2), blk(g)],
                     s_half.at[4 * g + k], r_half.at[4 * g + k], sibling) for ref, k in refs]

    lax.fori_loop(0, 4, outer, 0)
    for _s in solve_row(4, 3):
        pass

    def pcols(m, _):
        o = pl.ds(pl.multiple_of(m * 256, 256), 256)
        for j in range(0, n, 256):
            w = j + 256
            a = dot3((kch[o, :w], kcl[o, :w]), (xh[j + 256:w + 256, :w], xl[j + 256:w + 256, :w]), NT)
            ph[o, j:w], plo[o, j:w] = split(a)
        for j in range(0, n, 256):
            w = j + 256
            a = dot3((ph[o, j:], plo[o, j:]), (xh[j + 256:, j:w], xl[j + 256:, j:w]), NN)
            zh[o, j:w], zl[o, j:w] = split(a)
        return 0

    lax.fori_loop(0, cols_ref.shape[0] // 256, pcols, 0)
    lead_rows = pl.ds(pl.multiple_of(q * 64 + 256, 64), 64)
    keep = lax.broadcasted_iota(jnp.int32, (64, n), 1) <= q * 64 + lax.broadcasted_iota(jnp.int32, (64, n), 0)
    zh[:64, :] = jnp.where(keep, -xh[lead_rows, :].astype(f32), 0.0).astype(bf16)
    zl[:64, :] = jnp.where(keep, -xl[lead_rows, :].astype(f32), 0.0).astype(bf16)

    for g in range(4):
        for c in halves(g, core):
            c.wait_send()
        for c in halves(g, 1 - core):
            c.wait_recv()
    for c in leads + passed + half + rowsf + cols:
        c.wait_send()

    def last(m, _):
        o = pl.ds(pl.multiple_of(m * 256, 256), 256)
        out[o, :] = ktr[o, :] - dot3((krh[o, :], krl[o, :]), (zh[...], zl[...]), NT)
        return 0

    lax.fori_loop(0, rows_ref.shape[0] // 256, last, 0)


def fused(pool, ids, rot):
    n = pool.shape[0]
    c = n // 2
    dma = pltpu.SemaphoreType.DMA
    v = pltpu.VMEM
    return pl.pallas_call(
        fused_kernel,
        out_shape=jax.ShapeDtypeStruct((n, c), f32),
        in_specs=[VMEM] * 4,
        out_specs=VMEM,
        scratch_shapes=[
            v((n, E), bf16), v((c, E), bf16), v((4, n, F), bf16), v((n + c, 128), bf16), v((n, E), bf16), v((n, E), bf16),
            v((n + 256, n), f32), v((n + 256, n), bf16), v((n + 256, n), bf16), v((256, 256), bf16), v((256, 256), bf16),
            v((256, 256), f32), v((4, c, F), bf16), v((n, n), bf16), v((n, n), bf16), v((c, n), bf16), v((c, n), bf16),
            v((n, c), f32), v((2, 256, 256), f32), v((c, n), bf16), v((c, n), bf16), v((c, n), bf16), v((c, n), bf16),
            dma((3,)), dma((G - 1,)), dma((1,)), dma((G - 1,)), dma((8,)), dma((7,)), dma((7,)), dma((8,)), dma((G - 1,)),
            dma((G - 1,)), dma((G - 1,)), dma((G - 1,)), dma((8,)), dma((8,)), dma((16,)), dma((16,)),
        ],
        compiler_params=pltpu.CompilerParams(collective_id=0, has_side_effects=True, vmem_limit_bytes=ROOM),
    )(pool, ids.reshape(n // 128, 128), rot.reshape(n // 128, 128), jnp.asarray(bin_table()))


def solution(mesh):
    return jax.shard_map(
        fused,
        mesh=mesh,
        in_specs=(P("row", None), P("row", None), P("row")),
        out_specs=P("row", "col"),
        check_vma=False,
    )
```

time: 126 us -> 110 us (0.87)
  Pallas kernels: 125 us -> 105 us
  local copies, waits for them, and re-layouts: 0 us -> 3.08 us
    pallas_call x2 -> x1, Pallas kernels: 125 us -> 105 us  [fused(): pl.pallas_call(fused_kernel, out_shape=jax.ShapeDtypeStruct((n, c), f32),...]
    unnamed x0 -> x1, local copies, waits for them, and re-layouts: none -> 3.08 us
where the time goes in v4:
time: 110 us; the launch traced here: 108 us
  Pallas kernels  105 us (95%)
  local copies, waits for them, and re-layouts  3.08 us (3%)
    pallas_call x1, Pallas kernels, fused(): pl.pallas_call(fused_kernel, out_shape=jax.ShapeDtypeStruct((n, c), f32),...  105 us
    unnamed x1, local copies, waits for them, and re-layouts  3.08 us

profile of v4, /device:TPU:102, one launch (start us, length us, event | category | flops | bytes accessed | tf_op | source)
XLA Modules:
  0.0 108.3 jit_solution(9917589561154614889)
XLA Ops:
  0.0 105.2 %shard_map.46 = f32[1024,512]{1,0:T(8,128)} custom-call(bf16[1024,512]{1,0:T(8,128)(2,1)} %pool_ref.1, s32[8,128]{1,0:T(8,128)} %bitcast.2, s32[8,128]{1,0:T(8,128)} %bitcast.3, bf16[128,128]{1,0:T(8,128)(2,1)} %constant.2.clone.table_ref), custom_call_target="tpu_custom_call" | custom-call | tf_op jit(solution)/shard_map/pallas_call | solution.py:499
  105.2 3.1 %copy.6 = f32[1024,512]{1,0:T(8,128)} copy(f32[1024,512]{1,0:T(8,128)} %shard_map.46) | data formatting | bytes 4194304
